TPU v7x, 128 devices: a whole 4x4x4 slice. The times are simulated.
128 devices in a mesh: dp: 32 (over y_hi, z, x), tensor: 4 (over y_lo, core).
Axes of the slice: x: 4, y: 4 (y_hi: 2, y_lo: 2; y = y_hi * 2 + y_lo), z: 4, core: 2. Of those that a mesh axis runs over, the one named last changes fastest.
Arguments:
- tokens: bfloat16 [4608, 1024], P('dp', 'tensor'), may hold values from -6 to 6
- lengths: int32 [32, 4], P('dp'), may hold values from 1 to 72, 144 in all within a row
- attn_gain: float32 [1024], replicated, may hold values from 0.25 to 1.75
- w_query: bfloat16 [1024, 1024], P(None, 'tensor'), may hold values from -0.1875 to 0.1875
- key_weight: bfloat16 [1024, 512], P(None, 'tensor'), may hold values from -0.1875 to 0.1875
- value_weight: bfloat16 [1024, 512], P(None, 'tensor'), may hold values from -0.1875 to 0.1875
- query_gain: float32 [64], replicated, may hold values from 0.25 to 1.75
- key_gain: float32 [64], replicated, may hold values from 0.25 to 1.75
- w_output: bfloat16 [1024, 1024], P('tensor'), may hold values from -1 to 1
- mlp_gain: float32 [1024], replicated, may hold values from 0.25 to 1.75
- w_gate: bfloat16 [1024, 4608], P(None, 'tensor'), may hold values from -0.1875 to 0.1875
- w_up: bfloat16 [1024, 4608], P(None, 'tensor'), may hold values from -0.1875 to 0.1875
- w_down: bfloat16 [4608, 1024], P('tensor'), may hold values from -0.1875 to 0.1875
- cotangent: bfloat16 [4608, 1024], P('dp', 'tensor'), may hold values from -6 to 6
Outputs:
- block_out: bfloat16 [4608, 1024], P('dp', 'tensor')
- input_grad: bfloat16 [4608, 1024], P('dp', 'tensor')
- attn_gain_grad: float32 [1024], replicated
- w_query_grad: float32 [1024, 1024], P(None, 'tensor')
- w_key_grad: float32 [1024, 512], P(None, 'tensor')
- w_value_grad: float32 [1024, 512], P(None, 'tensor')
- query_gain_grad: float32 [64], replicated
- key_gain_grad: float32 [64], replicated
- w_output_grad: float32 [1024, 1024], P('tensor')
- mlp_gain_grad: float32 [1024], replicated
- w_gate_grad: float32 [1024, 4608], P(None, 'tensor')
- w_up_grad: float32 [1024, 4608], P(None, 'tensor')
- w_down_grad: float32 [4608, 1024], P('tensor')
Inputs may be any that keep to these rules, and one draw needn't show every extreme that they name: `lengths`: each row sums to 144, and its largest entry is exactly 72.
All inputs are finite; a program needn't handle non-finite values.
Results may differ from a plain program's by a relative error of at most 0.035.
Values may be sent and summed in bfloat16 or wider, within the bound.
A program may use at most 128 MiB of HBM per device.

v0:
```python
import jax
import jax.numpy as jnp
from jax import lax
from jax.sharding import PartitionSpec as P

HEAD_SIZE = 64


EPS = 1e-05
THETA = 1000000.0


def dot_rows(left_side, right_side):
    return lax.dot_general(
        left_side, right_side, (((0,), (0,)), ((), ())), preferred_element_type=jnp.float32
    )


def dot_last(left_side, right_side):
    return lax.dot_general(
        left_side, right_side, (((1,), (1,)), ((), ())), preferred_element_type=jnp.float32
    )


def layout(row_lengths, row_count):
    row_index = jnp.arange(row_count, dtype=jnp.int32)
    seq_ends = jnp.cumsum(row_lengths)
    segment_index = jnp.sum((row_index[:, None] >= seq_ends[None, :]).astype(jnp.int32), axis=1)
    starts = seq_ends - row_lengths
    choose = segment_index[:, None] == jnp.arange(row_lengths.shape[0], dtype=jnp.int32)[None, :]
    picked = jnp.sum(jnp.where(choose, starts[None, :], 0), axis=1)
    return (segment_index, row_index - picked)


def rotary_tables(position):
    half_width = HEAD_SIZE // 2
    frequency = THETA ** (-jnp.arange(half_width, dtype=jnp.float32) * 2.0 / HEAD_SIZE)
    angles = position.astype(jnp.float32)[:, None] * frequency[None, :]
    return (jnp.cos(angles), jnp.sin(angles))


def rotate(value_rows, cosine, sine_table):
    half_width = value_rows.shape[-1] // 2
    first_half = value_rows[..., :half_width]
    second_half = value_rows[..., half_width:]
    cosine = cosine[:, None, :]
    sine_table = sine_table[:, None, :]
    return jnp.concatenate(
        [
            first_half * cosine - second_half * sine_table,
            second_half * cosine + first_half * sine_table,
        ],
        axis=-1,
    )


def norm_back(upstream, plain_values, inverse):
    return inverse * (
        upstream - plain_values * jnp.mean(upstream * plain_values, axis=-1, keepdims=True)
    )


def body(
    tokens,
    lengths,
    attn_gain,
    w_query,
    key_weight,
    value_weight,
    query_gain,
    key_gain,
    w_output,
    mlp_gain,
    w_gate,
    w_up,
    w_down,
    cotangent,
):
    score_scale = HEAD_SIZE ** (-0.5)
    whole_tokens, whole_cot = (
        lax.all_gather(tokens, "tensor", axis=1, tiled=True),
        lax.all_gather(cotangent, "tensor", axis=1, tiled=True),
    )
    row_count = whole_tokens.shape[0]
    head_count = w_query.shape[1] // HEAD_SIZE
    groups = key_weight.shape[1] // HEAD_SIZE
    shared = head_count // groups
    segment_index, position = layout(lengths[0], row_count)
    row_index = jnp.arange(row_count, dtype=jnp.int32)
    allowed = (
        (segment_index[:, None] == segment_index[None, :])
        & (row_index[:, None] >= row_index[None, :])
    )[None, None]
    cosine, sine_table = rotary_tables(position)
    resid = whole_tokens.astype(jnp.float32)
    inverse_one = lax.rsqrt(jnp.mean(resid * resid, axis=-1, keepdims=True) + EPS)
    plain_one = resid * inverse_one
    first_normed_input = (plain_one * attn_gain).astype(jnp.bfloat16)
    query_raw = jnp.dot(first_normed_input, w_query, preferred_element_type=jnp.float32).reshape(
        row_count, head_count, HEAD_SIZE
    )
    key_unrotated = jnp.dot(
        first_normed_input, key_weight, preferred_element_type=jnp.float32
    ).reshape(row_count, groups, HEAD_SIZE)
    value_low = (
        jnp.dot(first_normed_input, value_weight, preferred_element_type=jnp.float32)
        .astype(jnp.bfloat16)
        .reshape(row_count, groups, HEAD_SIZE)
    )
    query_inverse = lax.rsqrt(jnp.mean(query_raw * query_raw, axis=-1, keepdims=True) + EPS)
    query_plain = query_raw * query_inverse
    query_low = (
        rotate(query_plain * query_gain, cosine, sine_table)
        .astype(jnp.bfloat16)
        .reshape(row_count, groups, shared, HEAD_SIZE)
    )
    key_inverse = lax.rsqrt(jnp.mean(key_unrotated * key_unrotated, axis=-1, keepdims=True) + EPS)
    key_plain = key_unrotated * key_inverse
    key_low = rotate(key_plain * key_gain, cosine, sine_table).astype(jnp.bfloat16)

    def score_block():
        raw_scores = (
            jnp.einsum("qjgd,kjd->jgqk", query_low, key_low, preferred_element_type=jnp.float32)
            * score_scale
        )
        return jnp.where(allowed, raw_scores, -1e30)

    scores = score_block()
    row_peak = jnp.max(scores, axis=-1, keepdims=True)
    weights = jnp.exp(scores - row_peak)
    denominator = jnp.sum(weights, axis=-1, keepdims=True)
    probs_low = (weights / denominator).astype(jnp.bfloat16)
    log_total = row_peak + jnp.log(denominator)
    heads_out = (
        jnp.einsum("jgqk,kjd->qjgd", probs_low, value_low, preferred_element_type=jnp.float32)
        .astype(jnp.bfloat16)
        .reshape(row_count, head_count * HEAD_SIZE)
    )
    attn_part = jnp.dot(heads_out, w_output, preferred_element_type=jnp.float32)
    hidden = resid + lax.psum(attn_part.astype(jnp.bfloat16), "tensor").astype(jnp.float32)
    inverse_two = lax.rsqrt(jnp.mean(hidden * hidden, axis=-1, keepdims=True) + EPS)
    plain_two = hidden * inverse_two
    normed_two = (plain_two * mlp_gain).astype(jnp.bfloat16)
    gate_proj = jnp.dot(normed_two, w_gate, preferred_element_type=jnp.float32)
    up_proj = jnp.dot(normed_two, w_up, preferred_element_type=jnp.float32)
    gate_sigmoid = jax.nn.sigmoid(gate_proj)
    activation = (gate_proj * gate_sigmoid * up_proj).astype(jnp.bfloat16)
    mlp_part = jnp.dot(activation, w_down, preferred_element_type=jnp.float32)
    mlp_own = lax.psum_scatter(
        mlp_part.astype(jnp.bfloat16), "tensor", scatter_dimension=1, tiled=True
    ).astype(jnp.float32)
    own_width = tokens.shape[1]
    column = lax.axis_index("tensor") * own_width
    block_out = (lax.dynamic_slice_in_dim(hidden, column, own_width, 1) + mlp_own).astype(
        jnp.bfloat16
    )
    w_down_grad = dot_rows(activation, whole_cot)
    d_act = dot_last(whole_cot, w_down)
    d_gate_low = (d_act * up_proj * gate_sigmoid * (1.0 + gate_proj * (1.0 - gate_sigmoid))).astype(
        jnp.bfloat16
    )
    d_up_low = (d_act * gate_proj * gate_sigmoid).astype(jnp.bfloat16)
    w_gate_grad = dot_rows(normed_two, d_gate_low)
    w_up_grad = dot_rows(normed_two, d_up_low)
    d_two_part = dot_last(d_gate_low, w_gate) + dot_last(d_up_low, w_up)
    d_two = lax.psum(d_two_part.astype(jnp.bfloat16), "tensor").astype(jnp.float32)
    mlp_gain_grad = jnp.sum(d_two * plain_two, axis=0)
    d_hidden = whole_cot.astype(jnp.float32) + norm_back(d_two * mlp_gain, plain_two, inverse_two)
    mlp_sums = (mlp_gain_grad, w_gate_grad, w_up_grad, w_down_grad)
    d_hidden_low = d_hidden.astype(jnp.bfloat16)
    w_output_grad = dot_rows(heads_out, d_hidden_low)
    d_heads = (
        dot_last(d_hidden_low, w_output)
        .astype(jnp.bfloat16)
        .reshape(row_count, groups, shared, HEAD_SIZE)
    )
    probs = jnp.exp(score_block() - log_total)
    probs_back = probs.astype(jnp.bfloat16)
    d_value_low = (
        jnp.einsum("jgqk,qjgd->kjd", probs_back, d_heads, preferred_element_type=jnp.float32)
        .astype(jnp.bfloat16)
        .reshape(row_count, groups * HEAD_SIZE)
    )
    d_probs = jnp.einsum("qjgd,kjd->jgqk", d_heads, value_low, preferred_element_type=jnp.float32)
    d_scores_low = (probs * (d_probs - jnp.sum(d_probs * probs, axis=-1, keepdims=True))).astype(
        jnp.bfloat16
    )
    d_query_post = (
        jnp.einsum(
            "jgqk,kjd->qjgd", d_scores_low, key_low, preferred_element_type=jnp.float32
        ).reshape(row_count, head_count, HEAD_SIZE)
        * score_scale
    )
    d_key_post = (
        jnp.einsum("jgqk,qjgd->kjd", d_scores_low, query_low, preferred_element_type=jnp.float32)
        * score_scale
    )
    d_query_turn = rotate(d_query_post, cosine, -sine_table)
    d_key_turn = rotate(d_key_post, cosine, -sine_table)
    query_gain_part = jnp.sum(d_query_turn * query_plain, axis=(0, 1))
    key_gain_part = jnp.sum(d_key_turn * key_plain, axis=(0, 1))
    d_query_low = (
        norm_back(d_query_turn * query_gain, query_plain, query_inverse)
        .astype(jnp.bfloat16)
        .reshape(row_count, head_count * HEAD_SIZE)
    )
    d_key_low = (
        norm_back(d_key_turn * key_gain, key_plain, key_inverse)
        .astype(jnp.bfloat16)
        .reshape(row_count, groups * HEAD_SIZE)
    )
    w_query_grad = dot_rows(first_normed_input, d_query_low)
    w_key_grad = dot_rows(first_normed_input, d_key_low)
    w_value_grad = dot_rows(first_normed_input, d_value_low)
    d_one_part = (
        dot_last(d_query_low, w_query)
        + dot_last(d_key_low, key_weight)
        + dot_last(d_value_low, value_weight)
    )
    d_one, query_gain_grad, key_gain_grad = (
        lax.psum(d_one_part.astype(jnp.bfloat16), "tensor").astype(jnp.float32),
        lax.psum(query_gain_part.astype(jnp.bfloat16), "tensor").astype(jnp.float32),
        lax.psum(key_gain_part.astype(jnp.bfloat16), "tensor").astype(jnp.float32),
    )
    attn_gain_grad = jnp.sum(d_one * plain_one, axis=0)
    d_input = d_hidden + norm_back(d_one * attn_gain, plain_one, inverse_one)
    input_grad = lax.dynamic_slice_in_dim(d_input, column, own_width, 1).astype(jnp.bfloat16)
    every_part = (
        lax.psum_scatter(
            attn_gain_grad.astype(jnp.bfloat16), "dp", scatter_dimension=0, tiled=True
        ).astype(jnp.float32),
        lax.psum_scatter(
            w_query_grad.astype(jnp.bfloat16), "dp", scatter_dimension=0, tiled=True
        ).astype(jnp.float32),
        lax.psum_scatter(
            w_key_grad.astype(jnp.bfloat16), "dp", scatter_dimension=0, tiled=True
        ).astype(jnp.float32),
        lax.psum_scatter(
            w_value_grad.astype(jnp.bfloat16), "dp", scatter_dimension=0, tiled=True
        ).astype(jnp.float32),
        lax.psum_scatter(
            query_gain_grad.astype(jnp.bfloat16), "dp", scatter_dimension=0, tiled=True
        ).astype(jnp.float32),
        lax.psum_scatter(
            key_gain_grad.astype(jnp.bfloat16), "dp", scatter_dimension=0, tiled=True
        ).astype(jnp.float32),
        lax.psum_scatter(
            w_output_grad.astype(jnp.bfloat16), "dp", scatter_dimension=0, tiled=True
        ).astype(jnp.float32),
        lax.psum_scatter(
            mlp_sums[0].astype(jnp.bfloat16), "dp", scatter_dimension=0, tiled=True
        ).astype(jnp.float32),
        lax.psum_scatter(
            mlp_sums[1].astype(jnp.bfloat16), "dp", scatter_dimension=0, tiled=True
        ).astype(jnp.float32),
        lax.psum_scatter(
            mlp_sums[2].astype(jnp.bfloat16), "dp", scatter_dimension=0, tiled=True
        ).astype(jnp.float32),
        lax.psum_scatter(
            mlp_sums[3].astype(jnp.bfloat16), "dp", scatter_dimension=0, tiled=True
        ).astype(jnp.float32),
    )
    summed = (
        lax.all_gather(every_part[0].astype(jnp.bfloat16), "dp", axis=0, tiled=True).astype(
            jnp.float32
        ),
        lax.all_gather(every_part[1].astype(jnp.bfloat16), "dp", axis=0, tiled=True).astype(
            jnp.float32
        ),
        lax.all_gather(every_part[2].astype(jnp.bfloat16), "dp", axis=0, tiled=True).astype(
            jnp.float32
        ),
        lax.all_gather(every_part[3].astype(jnp.bfloat16), "dp", axis=0, tiled=True).astype(
            jnp.float32
        ),
        lax.all_gather(every_part[4].astype(jnp.bfloat16), "dp", axis=0, tiled=True).astype(
            jnp.float32
        ),
        lax.all_gather(every_part[5].astype(jnp.bfloat16), "dp", axis=0, tiled=True).astype(
            jnp.float32
        ),
        lax.all_gather(every_part[6].astype(jnp.bfloat16), "dp", axis=0, tiled=True).astype(
            jnp.float32
        ),
        lax.all_gather(every_part[7].astype(jnp.bfloat16), "dp", axis=0, tiled=True).astype(
            jnp.float32
        ),
        lax.all_gather(every_part[8].astype(jnp.bfloat16), "dp", axis=0, tiled=True).astype(
            jnp.float32
        ),
        lax.all_gather(every_part[9].astype(jnp.bfloat16), "dp", axis=0, tiled=True).astype(
            jnp.float32
        ),
        lax.all_gather(every_part[10].astype(jnp.bfloat16), "dp", axis=0, tiled=True).astype(
            jnp.float32
        ),
    )
    attn_sums = summed[:7]
    mlp_sums = summed[7:]
    return (
        block_out,
        input_grad,
        attn_sums[0],
        attn_sums[1],
        attn_sums[2],
        attn_sums[3],
        attn_sums[4],
        attn_sums[5],
        attn_sums[6],
        mlp_sums[0],
        mlp_sums[1],
        mlp_sums[2],
        mlp_sums[3],
    )


def solution(mesh):
    in_specs = (
        P("dp", "tensor"),
        P("dp", None),
        P(),
        P(None, "tensor"),
        P(None, "tensor"),
        P(None, "tensor"),
        P(),
        P(),
        P("tensor", None),
        P(),
        P(None, "tensor"),
        P(None, "tensor"),
        P("tensor", None),
        P("dp", "tensor"),
    )
    out_specs = (
        P("dp", "tensor"),
        P("dp", "tensor"),
        P(),
        P(None, "tensor"),
        P(None, "tensor"),
        P(None, "tensor"),
        P(),
        P(),
        P("tensor", None),
        P(),
        P(None, "tensor"),
        P(None, "tensor"),
        P("tensor", None),
    )
    return jax.shard_map(body, mesh=mesh, in_specs=in_specs, out_specs=out_specs, check_vma=False)
```

profile of v0, /device:TPU:0, one launch (start us, length us, event | category | flops | bytes accessed | tf_op | source)
XLA Modules:
  0.0 1593.4 jit_solution(15715217556505368078)
XLA Ops:
  7.3 6.4 all_gather.39
  30.0 6.5 all_gather.40
  36.5 32.3 %all-reduce.17.cloned.1.call-done = bf16[144,1024]{1,0:T(8,128)(2,1)} async-done(((bf16[144,1024]{1,0:T(8,128)(2,1)}), bf16[144,1024]{1,0:T(8,128)(2,1)}) %all-reduce.17.cloned.1.call-update) | async-done | bytes 294928 | tf_op jit(solution)/shard_map/psum | solution.py:140
  71.2 2.2 fusion.36
  79.8 3.3 convolution_convert_fusion.2
  94.5 3.3 convolution_convert_fusion.1
  98.0 19.3 %all-reduce.19.cloned.1.call-done = bf16[144,1024]{1,0:T(8,128)(2,1)} async-done(((bf16[144,1024]{1,0:T(8,128)(2,1)}), bf16[144,1024]{1,0:T(8,128)(2,1)}) %all-reduce.19.cloned.1.call-update) | async-done | bytes 294928 | tf_op jit(solution)/shard_map/psum | solution.py:166
  140.1 2.6 multiply_reduce_fusion.3
  152.8 2.3 convolution_convert_fusion.5
  161.4 3.2 convolution_convert_fusion
  166.0 112.3 %fusion = bf16[40,1024]{1,0:T(8,128)(2,1)S(1)} fusion(bf16[1152,1024]{1,0:T(8,128)(2,1)} %convolution_convert_fusion), kind=kCustom, calls=%all-reduce-scatter | all-reduce-scatter fusion | flops 1310721 | bytes 2441728
  285.6 6.5 concatenate.31
  293.7 58.6 %reduce-scatter.20.cloned.1.call-done = bf16[32,1152]{1,0:T(8,128)(2,1)} async-done(((bf16[1024,1152]{1,0:T(8,128)(2,1)}), bf16[32,1152]{1,0:T(8,128)(2,1)}) %reduce-scatter.20.cloned.1.call-update) | async-done | bytes 73744 | tf_op jit(solution)/shard_map/reduce_scatter | solution.py:253
  352.3 227.7 %reduce-scatter.22.cloned.1.call-done = bf16[32,1152]{1,0:T(8,128)(2,1)} async-done(((bf16[1024,1152]{1,0:T(8,128)(2,1)}), bf16[32,1152]{1,0:T(8,128)(2,1)}) %reduce-scatter.22.cloned.1.call-update) | async-done | bytes 73744 | tf_op jit(solution)/shard_map/reduce_scatter | solution.py:256
  582.9 33.0 %all-reduce.21.cloned.1.call-done = bf16[144,1024]{1,0:T(8,128)(2,1)} async-done(((bf16[144,1024]{1,0:T(8,128)(2,1)}), bf16[144,1024]{1,0:T(8,128)(2,1)}) %all-reduce.21.cloned.1.call-update) | async-done | bytes 294928 | tf_op jit(solution)/shard_map/psum | solution.py:221
  615.9 2.2 fusion.14
  618.1 97.1 %all-reduce.11 = (bf16[1024]{0:T(1024)(128)(2,1)S(1)}, bf16[64]{0:T(256)(128)(2,1)S(1)}, bf16[64]{0:T(256)(128)(2,1)S(1)}, bf16[1024]{0:T(1024)(128)(2,1)S(1)}) all-reduce(bf16[1024]{0:T(1024)(128)(2,1)S(1)} %get-tuple-element.15, bf16[64]{0:T(256)(128)(2,1)S(1)} %reduce_sum.173, ...), channel_id=3, replica_groups=mesh['dp'=32,'tensor'=4] {'dp'}, use_global_device_ids=true, to_apply=%region_19.20.clone | all-reduce | flops 2176 | bytes 8704
  715.4 5.7 all-reduce.12
  722.1 89.9 %all-reduce.10 = (bf16[1024]{0:T(1024)(128)(2,1)S(1)}, bf16[64]{0:T(256)(128)(2,1)S(1)}, bf16[64]{0:T(256)(128)(2,1)S(1)}, bf16[1024]{0:T(1024)(128)(2,1)S(1)}) all-reduce(bf16[1024]{0:T(1024)(128)(2,1)S(1)} %dynamic-update-slice, bf16[64]{0:T(256)(128)(2,1)S(1)} %dynamic-update-slice.1, ...), channel_id=1, replica_groups=mesh['dp'=32,'tensor'=4] {'dp'}, use_global_device_ids=true, to_apply=%add | all-reduce | flops 2176 | bytes 8704
  817.6 6.7 reduce-scatter.16.cloned.1.call-done
  824.2 89.7 %all_gather.44 = bf16[1024,128]{1,0:T(8,128)(2,1)S(1)} all-gather(bf16[32,128]{1,0:T(8,128)(2,1)} %reduce-scatter.16.cloned.1.call-done), channel_id=1, replica_groups=mesh['dp'=32,'tensor'=4] {'dp'}, dimensions={0}, use_global_device_ids=true | all-gather | bytes 270336 | tf_op jit(solution)/shard_map/all_gather | solution.py:273
  914.8 90.4 %reduce-scatter.14.cloned.1.call-done = bf16[32,128]{1,0:T(8,128)(2,1)} async-done(((bf16[1024,128]{1,0:T(8,128)(2,1)}), bf16[32,128]{1,0:T(8,128)(2,1)}) %reduce-scatter.14.cloned.1.call-update) | async-done | bytes 8208 | tf_op jit(solution)/shard_map/reduce_scatter | solution.py:235
  1005.2 89.7 %all_gather.43 = bf16[1024,128]{1,0:T(8,128)(2,1)S(1)} all-gather(bf16[32,128]{1,0:T(8,128)(2,1)} %reduce-scatter.14.cloned.1.call-done), channel_id=1, replica_groups=mesh['dp'=32,'tensor'=4] {'dp'}, dimensions={0}, use_global_device_ids=true | all-gather | bytes 270336 | tf_op jit(solution)/shard_map/all_gather | solution.py:270
  1095.8 90.9 %reduce-scatter.18.cloned.1.call-done = bf16[8,1024]{1,0:T(8,128)(2,1)} async-done(((bf16[256,1024]{1,0:T(8,128)(2,1)}), bf16[8,1024]{1,0:T(8,128)(2,1)}) %reduce-scatter.18.cloned.1.call-update) | async-done | bytes 16400 | tf_op jit(solution)/shard_map/reduce_scatter | solution.py:247
  1186.7 91.3 %all_gather.47 = bf16[256,1024]{1,0:T(8,128)(2,1)S(1)} all-gather(bf16[8,1024]{1,0:T(8,128)(2,1)} %reduce-scatter.18.cloned.1.call-done), channel_id=1, replica_groups=mesh['dp'=32,'tensor'=4] {'dp'}, dimensions={0}, use_global_device_ids=true | all-gather | bytes 540672 | tf_op jit(solution)/shard_map/all_gather | solution.py:282
  1279.0 89.0 %reduce-scatter.12.cloned.1.call-done = bf16[32,256]{1,0:T(8,128)(2,1)} async-done(((bf16[1024,256]{1,0:T(8,128)(2,1)}), bf16[32,256]{1,0:T(8,128)(2,1)}) %reduce-scatter.12.cloned.1.call-update) | async-done | bytes 16400 | tf_op jit(solution)/shard_map/reduce_scatter | solution.py:232
  1368.1 91.7 %all_gather.42 = bf16[1024,256]{1,0:T(8,128)(2,1)S(1)} all-gather(bf16[32,256]{1,0:T(8,128)(2,1)} %reduce-scatter.12.cloned.1.call-done), channel_id=1, replica_groups=mesh['dp'=32,'tensor'=4] {'dp'}, dimensions={0}, use_global_device_ids=true | all-gather | bytes 540672 | tf_op jit(solution)/shard_map/all_gather | solution.py:267
  1460.9 4.5 reshape.288
  1465.3 45.6 %all-gather.5.cloned.1.call-done = bf16[1024,1152]{1,0:T(8,128)(2,1)} async-done(((bf16[32,1152]{1,0:T(8,128)(2,1)}), bf16[1024,1152]{1,0:T(8,128)(2,1)}) %all-gather.5.cloned.1.call-update) | async-done | bytes 2359312 | tf_op jit(solution)/shard_map/all_gather | solution.py:288
  1510.9 4.2 convert_element_type.242
  1515.1 67.6 %all-gather.7.cloned.1.call-done = bf16[1024,1152]{1,0:T(8,128)(2,1)} async-done(((bf16[32,1152]{1,0:T(8,128)(2,1)}), bf16[1024,1152]{1,0:T(8,128)(2,1)}) %all-gather.7.cloned.1.call-update) | async-done | bytes 2359312 | tf_op jit(solution)/shard_map/all_gather | solution.py:291
  1582.7 4.2 convert_element_type.244
  (252 shorter events, 95.2 us)
Async XLA Ops:
  7.2 66.9 %copy-start = (bf16[1152,1024]{1,0:T(8,128)(2,1)S(1)}, bf16[1152,1024]{1,0:T(8,128)(2,1)}, u32[]{:S(2)}) copy-start(bf16[1152,1024]{1,0:T(8,128)(2,1)} %param.26) | copy-start | bytes 7077892
  7.2 12.4 copy-start.44
  7.2 12.4 copy-start.24
  7.2 13.6 copy-start.47
  7.2 61.6 %all-reduce.17.cloned.1.call-start = ((), (), s32[]{:S(2)}) async-start(), calls=%async_computation.7 | async-start | bytes 589824 | tf_op jit(solution)/shard_map/psum | solution.py:140
  13.9 9.2 copy-start.38
  26.1 44.0 %copy-start.35 = (f32[2,2,144]{2,1,0:T(2,128)}, f32[2,2,144]{2,1,0:T(2,128)S(1)}, u32[]{:S(2)}) copy-start(f32[2,2,144]{2,1,0:T(2,128)S(1)} %fusion.16) | copy-start | bytes 6916
  26.1 44.0 %copy-start.34 = (f32[1024]{0:T(1024)S(1)}, f32[1024]{0:T(1024)}, u32[]{:S(2)}) copy-start(f32[1024]{0:T(1024)} %param.23) | copy-start | bytes 12292
  29.9 87.4 %all-reduce.19.cloned.1.call-start = ((), (), s32[]{:S(2)}) async-start(), calls=%async_computation.9 | async-start | bytes 589824 | tf_op jit(solution)/shard_map/psum | solution.py:166
  79.8 272.5 %reduce-scatter.20.cloned.1.call-start = ((), (), s32[]{:S(2)}) async-start(), calls=%async_computation.15 | async-start | bytes 2433024 | tf_op jit(solution)/shard_map/reduce_scatter | solution.py:253
  83.1 496.9 %reduce-scatter.22.cloned.1.call-start = ((), (), s32[]{:S(2)}) async-start(), calls=%async_computation.17 | async-start | bytes 2433024 | tf_op jit(solution)/shard_map/reduce_scatter | solution.py:256
  94.5 22.9 %copy-start.37 = (f32[144]{0:T(256)S(1)}, f32[144]{0:T(256)}, u32[]{:S(2)}) copy-start(f32[144]{0:T(256)} %copy-done.36) | copy-start | bytes 1732
  97.8 19.6 %copy-start.7 = (bf16[144,1024]{1,0:T(8,128)(2,1)S(1)}, bf16[144,1024]{1,0:T(8,128)(2,1)}, u32[]{:S(2)}) copy-start(bf16[144,1024]{1,0:T(8,128)(2,1)} %all-reduce.17.cloned.1.call-done) | copy-start | bytes 884740
  97.8 518.1 %all-reduce.21.cloned.1.call-start = ((), (), s32[]{:S(2)}) async-start(), calls=%async_computation.10 | async-start | bytes 589824 | tf_op jit(solution)/shard_map/psum | solution.py:221
  125.0 15.0 copy-start.6
  125.0 15.0 copy-start.42
  135.2 11.3 copy-start.49
  137.0 10.6 copy-start.46
  152.7 663.2 %reduce-scatter.10.cloned.1.call-start = ((), (), s32[]{:S(2)}) async-start(), calls=%async_computation.8 | async-start | bytes 368640 | tf_op jit(solution)/shard_map/reduce_scatter | solution.py:149
  155.1 669.1 %reduce-scatter.16.cloned.1.call-start = ((), (), s32[]{:S(2)}) async-start(), calls=%async_computation.13 | async-start | bytes 270336 | tf_op jit(solution)/shard_map/reduce_scatter | solution.py:238
  157.2 848.0 %reduce-scatter.14.cloned.1.call-start = ((), (), s32[]{:S(2)}) async-start(), calls=%async_computation.12 | async-start | bytes 270336 | tf_op jit(solution)/shard_map/reduce_scatter | solution.py:235
  159.2 1027.4 %reduce-scatter.18.cloned.1.call-start = ((), (), s32[]{:S(2)}) async-start(), calls=%async_computation.14 | async-start | bytes 540672 | tf_op jit(solution)/shard_map/reduce_scatter | solution.py:247
  161.3 1206.7 %reduce-scatter.12.cloned.1.call-start = ((), (), s32[]{:S(2)}) async-start(), calls=%async_computation.11 | async-start | bytes 540672 | tf_op jit(solution)/shard_map/reduce_scatter | solution.py:232
  164.6 119.6 %copy-start.43 = (u32[128]{0:T(128)S(1)}, u32[128]{0:T(128)}, u32[]{:S(2)}) copy-start(u32[128]{0:T(128)} %constant.54) | copy-start | bytes 1540
  166.0 452.1 %copy-start.40 = (bf16[1024]{0:T(1024)(128)(2,1)S(1)}, bf16[1024]{0:T(1024)(128)(2,1)}, u32[]{:S(2)}) copy-start(bf16[1024]{0:T(1024)(128)(2,1)} %get-tuple-element.13) | copy-start | bytes 6148
  166.0 1294.9 %all-gather.9.cloned.1.call-start = ((), (), s32[]{:S(2)}) async-start(), calls=%async_computation.19 | async-start | bytes 2703360 | tf_op jit(solution)/shard_map/all_gather | solution.py:294
  278.4 7.2 collective-permute-start.2
  279.7 5.9 collective-permute-start.1
  281.0 4.6 collective-permute-start
  282.9 2.6 collective-permute-start.3
  293.6 1217.3 %all-gather.5.cloned.1.call-start = ((), (), s32[]{:S(2)}) async-start(), calls=%async_computation.16 | async-start | bytes 2433024 | tf_op jit(solution)/shard_map/all_gather | solution.py:288
  352.3 1230.4 %all-gather.7.cloned.1.call-start = ((), (), s32[]{:S(2)}) async-start(), calls=%async_computation.18 | async-start | bytes 2433024 | tf_op jit(solution)/shard_map/all_gather | solution.py:291
  (35 other events, 114.0 us)
Sparse Core Ops, SparseCore 0:
  30.1 38.7 all-reduce.16
  79.9 37.4 all-reduce.18
  122.9 229.2 reduce-scatter.19
  357.7 222.2 reduce-scatter.21
  582.4 33.4 all-reduce.20
  618.7 18.3 reduce-scatter.9
  639.5 184.7 reduce-scatter.15
  826.7 178.4 reduce-scatter.13
  1007.6 179.0 reduce-scatter.17
  1189.0 179.0 reduce-scatter.11
  1371.7 67.5 all-gather.8
  1442.2 68.6 all-gather.4
  1514.0 68.6 all-gather.6
where the time goes:
time: 1600 us; the launch traced here: 1590 us
  waiting for transfers between devices  761 us (48%)
  blocking collectives  681 us (43%)
  local copies, waits for them, and re-layouts  44.7 us (3%)
  other arithmetic  41.9 us (3%)
  matrix products  40.3 us (3%)
  between operations  18 us (1%)
    unnamed x3, blocking collectives  299 us
    reduce_scatter x1, waiting for transfers between devices, body(): lax.psum_scatter(mlp_sums[2].astype(jnp.bfloat16), 'dp', scatter_dimensio...  228 us
    all_gather x1, blocking collectives, body(): lax.all_gather(every_part[1].astype(jnp.bfloat16), 'dp', axis=0, tiled=True)  91.7 us
    all_gather x1, blocking collectives, body(): lax.all_gather(every_part[6].astype(jnp.bfloat16), 'dp', axis=0, tiled=True)  91.3 us
    reduce_scatter x1, waiting for transfers between devices, body(): lax.psum_scatter(w_output_grad.astype(jnp.bfloat16), 'dp', scatter_dimens...  90.9 us
    reduce_scatter x1, waiting for transfers between devices, body(): lax.psum_scatter(w_key_grad.astype(jnp.bfloat16), 'dp', scatter_dimension...  90.4 us
    all_gather x1, blocking collectives, body(): lax.all_gather(every_part[3].astype(jnp.bfloat16), 'dp', axis=0, tiled=True)  89.7 us
    all_gather x1, blocking collectives, body(): lax.all_gather(every_part[2].astype(jnp.bfloat16), 'dp', axis=0, tiled=True)  89.7 us
  transfers between devices with their start and end apart: 17, of which 12 were waited for; matrix products, arithmetic and copies ran while one was open for 13% of the time, Pallas kernels for 0%

commit v1 on v0

--- a/solution.py
+++ b/solution.py
@@ -1,9 +1,418 @@
+import functools
 import jax
 import jax.numpy as jnp
 from jax import lax
+from jax.experimental import pallas as pl
+from jax.experimental.pallas import tpu as pltpu
 from jax.sharding import PartitionSpec as P
 
 HEAD_SIZE = 64
+MESH = pl.DeviceIdType.MESH
+
+
+def add_into(out, parts, step):
+    lead = out.shape[0]
+    rows = out.shape[1]
+    per = rows // step
+
+    def add_step(i, _):
+        b = i // per
+        r = pl.multiple_of((i % per) * step, 16)
+        total = parts[0][b, pl.ds(r, step), :].astype(jnp.float32)
+        for part in parts[1:]:
+            total = total + part[b, pl.ds(r, step), :].astype(jnp.float32)
+        out[b, pl.ds(r, step), :] = total.astype(jnp.bfloat16)
+        return 0
+
+    lax.fori_loop(0, lead * per, add_step, 0)
+
+
+COPIES = ("t1p", "t1m", "i1p", "i1m", "m1p", "m1m", "t2p", "t2m", "i2p", "i2m", "m2p", "m2m", "y", "a2p", "a2m", "f2p", "f2m", "a1p", "a1m", "f1p", "f1m")
+KEYS = len(COPIES)
+
+
+class Chunk:
+    def __init__(self, src, dst, t1, r1, m1, s1, t2, r2, m2, s2, yb, send, recv, step, where):
+        self.src, self.dst = src, dst
+        self.t1, self.r1, self.m1, self.s1 = t1, r1, m1, s1
+        self.t2, self.r2, self.m2, self.s2, self.yb = t2, r2, m2, s2, yb
+        self.send, self.recv, self.step = send, recv, step
+        y, z, x = where
+        self.where = where
+
+        def dev(yy, zz, xx):
+            return {"dp": (yy * 4 + zz) * 4 + xx}
+
+        up = lambda v: lax.rem(v + 1, 4)
+        down = lambda v: lax.rem(v + 3, 4)
+        xp, xm = dev(y, z, up(x)), dev(y, z, down(x))
+        zp, zm = dev(y, up(z), x), dev(y, down(z), x)
+        self.ynb = dev(1 - y, z, x)
+        self.first = ((x, xp, xm), (z, zp, zm))
+        self.second = ((z, zp, zm), (x, xp, xm))
+        self.live = {}
+
+    def go(self, h, name, src, dst, device):
+        k = h * KEYS + COPIES.index(name)
+        c = pltpu.make_async_remote_copy(
+            src_ref=src, dst_ref=dst, send_sem=self.send.at[k], recv_sem=self.recv.at[k],
+            device_id=device, device_id_type=MESH)
+        c.start()
+        self.live[h, name] = c
+
+    def got(self, h, *names):
+        for n in names:
+            self.live[h, n].wait_recv()
+
+    def start1(self):
+        for h in range(2):
+            p, plus, minus = self.first[h]
+            k2, kp, km = lax.rem(p + 2, 4), lax.rem(p + 1, 4), lax.rem(p + 3, 4)
+            H, T, R = self.src.at[h], self.t1.at[h], self.r1.at[h]
+            self.go(h, "t1p", H.at[k2, pl.ds(0, 2)], T.at[0], plus)
+            self.go(h, "t1m", H.at[k2, pl.ds(2, 2)], T.at[1], minus)
+            self.go(h, "i1p", H.at[kp, pl.ds(2, 2)], R.at[0, pl.ds(2, 2)], plus)
+            self.go(h, "i1m", H.at[km, pl.ds(0, 2)], R.at[1, pl.ds(0, 2)], minus)
+
+    def mid1(self):
+        for h in range(2):
+            p, plus, minus = self.first[h]
+            kp, km = lax.rem(p + 1, 4), lax.rem(p + 3, 4)
+            H, T, R, M = self.src.at[h], self.t1.at[h], self.r1.at[h], self.m1.at[h]
+            self.got(h, "t1p")
+            add_into(M.at[0], (H.at[kp, pl.ds(0, 2)], T.at[0]), self.step)
+            self.go(h, "m1p", M.at[0], R.at[0, pl.ds(0, 2)], plus)
+            self.got(h, "t1m")
+            add_into(M.at[1], (H.at[km, pl.ds(2, 2)], T.at[1]), self.step)
+            self.go(h, "m1m", M.at[1], R.at[1, pl.ds(2, 2)], minus)
+
+    def fin1(self):
+        for h in range(2):
+            p = self.first[h][0]
+            R = self.r1.at[h]
+            self.got(h, "i1p", "i1m", "m1p", "m1m")
+            add_into(self.s1.at[h], (self.src.at[h, p], R.at[0], R.at[1]), self.step)
+            p, plus, minus = self.second[h]
+            k2, kp, km = lax.rem(p + 2, 4), lax.rem(p + 1, 4), lax.rem(p + 3, 4)
+            H, T, R = self.s1.at[h], self.t2.at[h], self.r2.at[h]
+            half = T.shape[1]
+            lo, hi = pl.ds(0, half), pl.ds(half, half)
+            self.go(h, "t2p", H.at[k2, lo], T.at[0], plus)
+            self.go(h, "t2m", H.at[k2, hi], T.at[1], minus)
+            self.go(h, "i2p", H.at[kp, hi], R.at[0, hi], plus)
+            self.go(h, "i2m", H.at[km, lo], R.at[1, lo], minus)
+
+    def mid2(self):
+        for h in range(2):
+            p, plus, minus = self.second[h]
+            kp, km = lax.rem(p + 1, 4), lax.rem(p + 3, 4)
+            H, T, R, M = self.s1.at[h], self.t2.at[h], self.r2.at[h], self.m2.at[h]
+            half = T.shape[1]
+            lo, hi = pl.ds(0, half), pl.ds(half, half)
+            step = min(self.step, half)
+            self.got(h, "t2p")
+            add_into(M.at[pl.ds(0, 1)], (H.at[pl.ds(kp, 1), lo], T.at[pl.ds(0, 1)]), step)
+            self.go(h, "m2p", M.at[0], R.at[0, lo], plus)
+            self.got(h, "t2m")
+            add_into(M.at[pl.ds(1, 1)], (H.at[pl.ds(km, 1), hi], T.at[pl.ds(1, 1)]), step)
+            self.go(h, "m2m", M.at[1], R.at[1, hi], minus)
+
+    def fin2(self):
+        for h in range(2):
+            p = self.second[h][0]
+            R = self.r2.at[h]
+            self.got(h, "i2p", "i2m", "m2p", "m2m")
+            add_into(self.s2.at[pl.ds(h, 1)], (self.s1.at[h, pl.ds(p, 1)], R.at[pl.ds(0, 1)], R.at[pl.ds(1, 1)]), self.step)
+            self.go(h, "y", self.s2.at[h], self.yb.at[h], self.ynb)
+
+    def finy(self):
+        for h in range(2):
+            a = self.first[h][0]
+            p, plus, minus = self.second[h]
+            self.got(h, "y")
+            add_into(self.dst.at[h, a, pl.ds(p, 1)], (self.s2.at[pl.ds(h, 1)], self.yb.at[pl.ds(h, 1)]), self.step)
+            blk = self.dst.at[h, a, p]
+            self.go(h, "a2p", blk, blk, plus)
+            self.go(h, "a2m", blk, blk, minus)
+
+    def ag2(self):
+        for h in range(2):
+            a = self.first[h][0]
+            p, plus, minus = self.second[h]
+            kp, km = lax.rem(p + 1, 4), lax.rem(p + 3, 4)
+            half = self.t2.shape[2]
+            self.got(h, "a2p")
+            blk = self.dst.at[h, a, km, pl.ds(0, half)]
+            self.go(h, "f2p", blk, blk, plus)
+            self.got(h, "a2m")
+            blk = self.dst.at[h, a, kp, pl.ds(half, half)]
+            self.go(h, "f2m", blk, blk, minus)
+
+    def ag1s(self):
+        for h in range(2):
+            p, plus, minus = self.first[h]
+            self.got(h, "f2p", "f2m")
+            blk = self.dst.at[h, p]
+            self.go(h, "a1p", blk, blk, plus)
+            self.go(h, "a1m", blk, blk, minus)
+
+    def ag1(self):
+        for h in range(2):
+            p, plus, minus = self.first[h]
+            kp, km = lax.rem(p + 1, 4), lax.rem(p + 3, 4)
+            self.got(h, "a1p")
+            blk = self.dst.at[h, km, pl.ds(0, 2)]
+            self.go(h, "f1p", blk, blk, plus)
+            self.got(h, "a1m")
+            blk = self.dst.at[h, kp, pl.ds(2, 2)]
+            self.go(h, "f1m", blk, blk, minus)
+
+    def end(self):
+        for h in range(2):
+            self.got(h, "f1p", "f1m")
+        for c in self.live.values():
+            c.wait_send()
+
+    def stages(self):
+        return [self.start1, self.mid1, self.fin1, self.mid2, self.fin2, self.finy, self.ag2, self.ag1s, self.ag1, self.end]
+
+
+def run_chunks(chunks, lag=2):
+    todo = [c.stages() for c in chunks]
+    last = max(lag * i + len(t) for i, t in enumerate(todo))
+    for t in range(last):
+        ready = [(i, t - lag * i) for i in range(len(todo)) if 0 <= t - lag * i < len(todo[i])]
+        for i, s in ready:
+            if s == 0:
+                todo[i][s]()
+        for i, s in ready:
+            if s > 0:
+                todo[i][s]()
+
+
+def coords():
+    d = lax.axis_index("dp")
+    return d // 16, (d // 4) % 4, d % 4
+
+
+def scratch_for(shape):
+    _, _, _, R, C = shape
+    bf = jnp.bfloat16
+    return [
+        pltpu.VMEM((2, 2, 2, R, C), bf), pltpu.VMEM((2, 2, 4, R, C), bf), pltpu.VMEM((2, 2, 2, R, C), bf), pltpu.VMEM((2, 4, R, C), bf),
+        pltpu.VMEM((2, 2, R // 2, C), bf), pltpu.VMEM((2, 2, R, C), bf), pltpu.VMEM((2, 2, R // 2, C), bf), pltpu.VMEM((2, R, C), bf), pltpu.VMEM((2, R, C), bf),
+        pltpu.SemaphoreType.DMA((2 * KEYS,)), pltpu.SemaphoreType.DMA((2 * KEYS,)),
+    ]
+
+NS = 11
+
+def enter(y, z, x):
+    barrier = pltpu.get_barrier_semaphore()
+    peers = [(y, z, lax.rem(x + i, 4)) for i in (1, 2, 3)] + [(y, lax.rem(z + i, 4), x) for i in (1, 2, 3)] + [(1 - y, z, x)]
+    for a, b, c in peers:
+        pl.semaphore_signal(barrier, inc=1, device_id={"dp": (a * 4 + b) * 4 + c}, device_id_type=MESH)
+    pl.semaphore_wait(barrier, len(peers))
+
+
+def small_sum(where, vec, out, slots, mine, send, recv):
+    y, z, x = where
+    value = vec[...]
+    for s, (p, n, dev) in enumerate((
+        (x, 4, lambda v: (y * 4 + z) * 4 + v), (z, 4, lambda v: (y * 4 + v) * 4 + x), (y, 2, lambda v: (v * 4 + z) * 4 + x))):
+        mine[s] = value
+        slots[s, p] = value
+        cs = []
+        for i in range(1, n):
+            k = s * 3 + i - 1
+            c = pltpu.make_async_remote_copy(
+                src_ref=mine.at[s], dst_ref=slots.at[s, p], send_sem=send.at[k], recv_sem=recv.at[k],
+                device_id={"dp": dev(lax.rem(p + i, n))}, device_id_type=MESH)
+            c.start()
+            cs.append(c)
+        for c in cs:
+            c.wait()
+        value = slots[s, 0]
+        for i in range(1, n):
+            value = value + slots[s, i]
+    out[...] = value
+
+
+def reduce_kernel(n, steps, *refs):
+    ins, vec = refs[:n], refs[n]
+    outs, vout = refs[n + 1:2 * n + 1], refs[2 * n + 1]
+    rest = refs[2 * n + 2:]
+    where = coords()
+    enter(*where)
+    chunks = [Chunk(ins[i], outs[i], *rest[NS * i:NS * i + NS], steps[i], where) for i in range(n)]
+    if vec is not None:
+        small_sum(where, vec, vout, *rest[NS * n:])
+    run_chunks(chunks)
+
+
+def all_reduce(arrays, vec):
+    n = len(arrays)
+    shapes = [a.shape for a in arrays]
+    steps = [16 if s[-1] > 128 else s[-2] // 2 for s in shapes]
+    V = pl.BlockSpec(memory_space=pltpu.VMEM)
+    scratch = sum([scratch_for(s) for s in shapes], [])
+    scratch += [pltpu.VMEM((3, 4) + vec.shape, jnp.float32), pltpu.VMEM((3,) + vec.shape, jnp.float32),
+                pltpu.SemaphoreType.DMA((9,)), pltpu.SemaphoreType.DMA((9,))]
+    return pl.pallas_call(
+        functools.partial(reduce_kernel, n, steps),
+        out_shape=[jax.ShapeDtypeStruct(s, jnp.bfloat16) for s in shapes] + [jax.ShapeDtypeStruct(vec.shape, jnp.float32)],
+        in_specs=[V] * (n + 1), out_specs=[V] * (n + 1), scratch_shapes=scratch,
+        compiler_params=pltpu.CompilerParams(collective_id=0, has_side_effects=True, vmem_limit_bytes=60 * 1024 * 1024),
+        name="dp_sum",
+    )(*arrays, vec)
+
+
+def tensor_place():
+    t = lax.axis_index("tensor")
+    core, side = lax.rem(t, 2), t // 2
+    return side, core, side * 2 + (1 - core), (1 - side) * 2 + core
+
+
+def send(src, dst, sems, k, peer):
+    c = pltpu.make_async_remote_copy(
+        src_ref=src, dst_ref=dst, send_sem=sems[0].at[k], recv_sem=sems[1].at[k],
+        device_id={"tensor": peer}, device_id_type=MESH)
+    c.start()
+    return c
+
+
+def greet(sib, far):
+    barrier = pltpu.get_barrier_semaphore()
+    for peer in (sib, far):
+        pl.semaphore_signal(barrier, inc=1, device_id={"tensor": peer}, device_id_type=MESH)
+    pl.semaphore_wait(barrier, 2)
+
+
+def columns(block):
+    return pl.ds(pl.multiple_of(block * 256, 256), 256)
+
+
+def gather_kernel(a, b, oa, ob, s_sem, r_sem):
+    side, core, sib, far = tensor_place()
+    me = side * 2 + core
+    sems = (s_sem, r_sem)
+    greet(sib, far)
+    first = []
+    for i, (v, o) in enumerate(((a, oa), (b, ob))):
+        there = o.at[:, columns(me)]
+        first.append((send(v, there, sems, 3 * i, far), send(v, there, sems, 3 * i + 1, sib)))
+    for v, o in ((a, oa), (b, ob)):
+        o[:, columns(me)] = v[...]
+    passed = []
+    for i, o in enumerate((oa, ob)):
+        first[i][0].wait_recv()
+        there = o.at[:, columns(far)]
+        passed.append(send(there, there, sems, 3 * i + 2, sib))
+    for i in range(2):
+        first[i][0].wait_send()
+        first[i][1].wait()
+        passed[i].wait()
+
+
+def gather_pair(a, b):
+    V = pl.BlockSpec(memory_space=pltpu.VMEM)
+    shape = jax.ShapeDtypeStruct((a.shape[0], 4 * a.shape[1]), a.dtype)
+    return pl.pallas_call(
+        gather_kernel, out_shape=[shape, shape], in_specs=[V, V], out_specs=[V, V],
+        scratch_shapes=[pltpu.SemaphoreType.DMA((6,)), pltpu.SemaphoreType.DMA((6,))],
+        compiler_params=pltpu.CompilerParams(collective_id=1, has_side_effects=True), name="gather_pair",
+    )(a, b)
+
+
+def sum_steps(part, out, low, near, mid, away, sems, base, place, scatter):
+    side, core, sib, far = place
+    live = []
+
+    def one():
+        low[...] = part[...].astype(jnp.bfloat16)
+        for s in range(2):
+            live.append(send(low.at[:, columns(s * 2 + 1 - core)], near.at[s], sems, base + s, sib))
+
+    def two():
+        order = (1 - side, side)
+        for s in range(2):
+            live[s].wait_recv()
+        for i, s in enumerate(order):
+            mid[s] = (low[:, columns(s * 2 + core)].astype(jnp.float32) + near[s].astype(jnp.float32)).astype(jnp.bfloat16)
+            if i == 0 or not scatter:
+                live.append(send(mid.at[s], away.at[s], sems, base + 2 + i, far))
+
+    def three():
+        if scatter:
+            live[2].wait_recv()
+            out[...] = mid[side].astype(jnp.float32) + away[side].astype(jnp.float32)
+            return
+        for i, s in enumerate((1 - side, side)):
+            live[2 + i].wait_recv()
+        for i, s in enumerate((1 - side, side)):
+            there = out.at[:, columns(s * 2 + core)]
+            out[:, columns(s * 2 + core)] = (mid[s].astype(jnp.float32) + away[s].astype(jnp.float32)).astype(jnp.bfloat16)
+            live.append(send(there, there, sems, base + 4 + i, sib))
+
+    def four():
+        for c in live[4:]:
+            c.wait_recv()
+        for c in live:
+            c.wait_send()
+
+    return [one, two, three, four]
+
+
+def sums_kernel(kinds, *refs):
+    n = len(kinds)
+    ins, outs, rest = refs[:n], refs[n:2 * n], refs[2 * n:]
+    sems = rest[-2:]
+    place = tensor_place()
+    side, core, sib, far = place
+    greet(sib, far)
+    plans = []
+    for i, kind in enumerate(kinds):
+        if kind == "small":
+            near, mid, away = rest[4 * i + 1:4 * i + 4]
+            hold = []
+
+            def one(v=ins[i], near=near, k=6 * i, hold=hold):
+                hold.append(send(v, near, sems, k, sib))
+
+            def two(v=ins[i], near=near, mid=mid, away=away, k=6 * i, hold=hold):
+                hold[0].wait()
+                mid[...] = v[...] + near[...]
+                hold.append(send(mid, away, sems, k + 1, far))
+
+            def three(o=outs[i], mid=mid, away=away, hold=hold):
+                hold[1].wait()
+                o[...] = mid[...] + away[...]
+
+            plans.append([one, two, three, lambda: None])
+        else:
+            plans.append(sum_steps(ins[i], outs[i], *rest[4 * i:4 * i + 4], sems, 6 * i, place, kind == "own"))
+    for step in range(4):
+        for plan in plans:
+            plan[step]()
+
+
+def tensor_sums(arrays, kinds, collective_id):
+    V = pl.BlockSpec(memory_space=pltpu.VMEM)
+    out_shape, scratch = [], []
+    for a, kind in zip(arrays, kinds):
+        r, w = a.shape
+        if kind == "small":
+            out_shape.append(jax.ShapeDtypeStruct((r, w), jnp.float32))
+            scratch += [pltpu.VMEM((r, w), jnp.float32)] * 4
+        else:
+            out_shape.append(jax.ShapeDtypeStruct((r, w), jnp.bfloat16) if kind == "all" else jax.ShapeDtypeStruct((r, w // 4), jnp.float32))
+            scratch += [pltpu.VMEM((r, w), jnp.bfloat16)] + [pltpu.VMEM((2, r, w // 4), jnp.bfloat16)] * 3
+    n = len(arrays)
+    scratch += [pltpu.SemaphoreType.DMA((6 * n,)), pltpu.SemaphoreType.DMA((6 * n,))]
+    return pl.pallas_call(
+        functools.partial(sums_kernel, kinds), out_shape=out_shape, in_specs=[V] * n, out_specs=[V] * n,
+        scratch_shapes=scratch,
+        compiler_params=pltpu.CompilerParams(collective_id=collective_id, has_side_effects=True), name="tensor_sums",
+    )(*arrays)
 
 
 EPS = 1e-05
@@ -77,10 +486,7 @@
     cotangent,
 ):
     score_scale = HEAD_SIZE ** (-0.5)
-    whole_tokens, whole_cot = (
-        lax.all_gather(tokens, "tensor", axis=1, tiled=True),
-        lax.all_gather(cotangent, "tensor", axis=1, tiled=True),
-    )
+    whole_tokens, whole_cot = gather_pair(tokens, cotangent)
     row_count = whole_tokens.shape[0]
     head_count = w_query.shape[1] // HEAD_SIZE
     groups = key_weight.shape[1] // HEAD_SIZE
@@ -137,7 +543,7 @@
         .reshape(row_count, head_count * HEAD_SIZE)
     )
     attn_part = jnp.dot(heads_out, w_output, preferred_element_type=jnp.float32)
-    hidden = resid + lax.psum(attn_part.astype(jnp.bfloat16), "tensor").astype(jnp.float32)
+    hidden = resid + tensor_sums([attn_part], ("all",), 2)[0].astype(jnp.float32)
     inverse_two = lax.rsqrt(jnp.mean(hidden * hidden, axis=-1, keepdims=True) + EPS)
     plain_two = hidden * inverse_two
     normed_two = (plain_two * mlp_gain).astype(jnp.bfloat16)
@@ -146,15 +552,10 @@
     gate_sigmoid = jax.nn.sigmoid(gate_proj)
     activation = (gate_proj * gate_sigmoid * up_proj).astype(jnp.bfloat16)
     mlp_part = jnp.dot(activation, w_down, preferred_element_type=jnp.float32)
-    mlp_own = lax.psum_scatter(
-        mlp_part.astype(jnp.bfloat16), "tensor", scatter_dimension=1, tiled=True
-    ).astype(jnp.float32)
     own_width = tokens.shape[1]
     column = lax.axis_index("tensor") * own_width
-    block_out = (lax.dynamic_slice_in_dim(hidden, column, own_width, 1) + mlp_own).astype(
-        jnp.bfloat16
-    )
-    w_down_grad = dot_rows(activation, whole_cot)
+    w_down_grad = dot_rows(activation, whole_cot).astype(jnp.bfloat16)
+    w_down_blocks = w_down_grad.reshape(1152, 8, 128).transpose(1, 0, 2).reshape(2, 4, 4, 288, 128)
     d_act = dot_last(whole_cot, w_down)
     d_gate_low = (d_act * up_proj * gate_sigmoid * (1.0 + gate_proj * (1.0 - gate_sigmoid))).astype(
         jnp.bfloat16
@@ -163,12 +564,15 @@
     w_gate_grad = dot_rows(normed_two, d_gate_low)
     w_up_grad = dot_rows(normed_two, d_up_low)
     d_two_part = dot_last(d_gate_low, w_gate) + dot_last(d_up_low, w_up)
-    d_two = lax.psum(d_two_part.astype(jnp.bfloat16), "tensor").astype(jnp.float32)
+    d_two, mlp_own = tensor_sums([d_two_part, mlp_part], ("all", "own"), 3)
+    d_two = d_two.astype(jnp.float32)
+    block_out = (lax.dynamic_slice_in_dim(hidden, column, own_width, 1) + mlp_own).astype(
+        jnp.bfloat16
+    )
     mlp_gain_grad = jnp.sum(d_two * plain_two, axis=0)
     d_hidden = whole_cot.astype(jnp.float32) + norm_back(d_two * mlp_gain, plain_two, inverse_two)
-    mlp_sums = (mlp_gain_grad, w_gate_grad, w_up_grad, w_down_grad)
     d_hidden_low = d_hidden.astype(jnp.bfloat16)
-    w_output_grad = dot_rows(heads_out, d_hidden_low)
+    w_output_turned = dot_rows(d_hidden_low, heads_out)
     d_heads = (
         dot_last(d_hidden_low, w_output)
         .astype(jnp.bfloat16)
@@ -217,100 +621,38 @@
         + dot_last(d_key_low, key_weight)
         + dot_last(d_value_low, value_weight)
     )
-    d_one, query_gain_grad, key_gain_grad = (
-        lax.psum(d_one_part.astype(jnp.bfloat16), "tensor").astype(jnp.float32),
-        lax.psum(query_gain_part.astype(jnp.bfloat16), "tensor").astype(jnp.float32),
-        lax.psum(key_gain_part.astype(jnp.bfloat16), "tensor").astype(jnp.float32),
-    )
+    gains = jnp.pad(jnp.concatenate([query_gain_part, key_gain_part])[None], ((0, 7), (0, 0)))
+    d_one, gains = tensor_sums([d_one_part, gains], ("all", "small"), 4)
+    d_one = d_one.astype(jnp.float32)
     attn_gain_grad = jnp.sum(d_one * plain_one, axis=0)
     d_input = d_hidden + norm_back(d_one * attn_gain, plain_one, inverse_one)
     input_grad = lax.dynamic_slice_in_dim(d_input, column, own_width, 1).astype(jnp.bfloat16)
-    every_part = (
-        lax.psum_scatter(
-            attn_gain_grad.astype(jnp.bfloat16), "dp", scatter_dimension=0, tiled=True
-        ).astype(jnp.float32),
-        lax.psum_scatter(
-            w_query_grad.astype(jnp.bfloat16), "dp", scatter_dimension=0, tiled=True
-        ).astype(jnp.float32),
-        lax.psum_scatter(
-            w_key_grad.astype(jnp.bfloat16), "dp", scatter_dimension=0, tiled=True
-        ).astype(jnp.float32),
-        lax.psum_scatter(
-            w_value_grad.astype(jnp.bfloat16), "dp", scatter_dimension=0, tiled=True
-        ).astype(jnp.float32),
-        lax.psum_scatter(
-            query_gain_grad.astype(jnp.bfloat16), "dp", scatter_dimension=0, tiled=True
-        ).astype(jnp.float32),
-        lax.psum_scatter(
-            key_gain_grad.astype(jnp.bfloat16), "dp", scatter_dimension=0, tiled=True
-        ).astype(jnp.float32),
-        lax.psum_scatter(
-            w_output_grad.astype(jnp.bfloat16), "dp", scatter_dimension=0, tiled=True
-        ).astype(jnp.float32),
-        lax.psum_scatter(
-            mlp_sums[0].astype(jnp.bfloat16), "dp", scatter_dimension=0, tiled=True
-        ).astype(jnp.float32),
-        lax.psum_scatter(
-            mlp_sums[1].astype(jnp.bfloat16), "dp", scatter_dimension=0, tiled=True
-        ).astype(jnp.float32),
-        lax.psum_scatter(
-            mlp_sums[2].astype(jnp.bfloat16), "dp", scatter_dimension=0, tiled=True
-        ).astype(jnp.float32),
-        lax.psum_scatter(
-            mlp_sums[3].astype(jnp.bfloat16), "dp", scatter_dimension=0, tiled=True
-        ).astype(jnp.float32),
-    )
-    summed = (
-        lax.all_gather(every_part[0].astype(jnp.bfloat16), "dp", axis=0, tiled=True).astype(
-            jnp.float32
-        ),
-        lax.all_gather(every_part[1].astype(jnp.bfloat16), "dp", axis=0, tiled=True).astype(
-            jnp.float32
-        ),
-        lax.all_gather(every_part[2].astype(jnp.bfloat16), "dp", axis=0, tiled=True).astype(
-            jnp.float32
-        ),
-        lax.all_gather(every_part[3].astype(jnp.bfloat16), "dp", axis=0, tiled=True).astype(
-            jnp.float32
-        ),
-        lax.all_gather(every_part[4].astype(jnp.bfloat16), "dp", axis=0, tiled=True).astype(
-            jnp.float32
-        ),
-        lax.all_gather(every_part[5].astype(jnp.bfloat16), "dp", axis=0, tiled=True).astype(
-            jnp.float32
-        ),
-        lax.all_gather(every_part[6].astype(jnp.bfloat16), "dp", axis=0, tiled=True).astype(
-            jnp.float32
-        ),
-        lax.all_gather(every_part[7].astype(jnp.bfloat16), "dp", axis=0, tiled=True).astype(
-            jnp.float32
-        ),
-        lax.all_gather(every_part[8].astype(jnp.bfloat16), "dp", axis=0, tiled=True).astype(
-            jnp.float32
-        ),
-        lax.all_gather(every_part[9].astype(jnp.bfloat16), "dp", axis=0, tiled=True).astype(
-            jnp.float32
-        ),
-        lax.all_gather(every_part[10].astype(jnp.bfloat16), "dp", axis=0, tiled=True).astype(
-            jnp.float32
-        ),
-    )
-    attn_sums = summed[:7]
-    mlp_sums = summed[7:]
+    vec = jnp.concatenate([attn_gain_grad.reshape(8, 128), mlp_gain_grad.reshape(8, 128), gains], axis=0)
+    attn_grads = jnp.concatenate([w_query_grad, w_key_grad, w_value_grad, w_output_turned], axis=1).astype(jnp.bfloat16)
+    down, gate, up, attn, vec = all_reduce(
+        [
+            w_down_blocks,
+            w_gate_grad.astype(jnp.bfloat16).reshape(2, 4, 4, 32, 1152),
+            w_up_grad.astype(jnp.bfloat16).reshape(2, 4, 4, 32, 1152),
+            attn_grads.reshape(2, 4, 4, 32, 768),
+        ],
+        vec,
+    )
+    attn = attn.reshape(1024, 768).astype(jnp.float32)
     return (
         block_out,
         input_grad,
-        attn_sums[0],
-        attn_sums[1],
-        attn_sums[2],
-        attn_sums[3],
-        attn_sums[4],
-        attn_sums[5],
-        attn_sums[6],
-        mlp_sums[0],
-        mlp_sums[1],
-        mlp_sums[2],
-        mlp_sums[3],
+        vec[:8].reshape(1024),
+        attn[:, :256],
+        attn[:, 256:384],
+        attn[:, 384:512],
+        vec[16, :64],
+        vec[16, 64:],
+        attn[:, 512:].T,
+        vec[8:16].reshape(1024),
+        gate.reshape(1024, 1152).astype(jnp.float32),
+        up.reshape(1024, 1152).astype(jnp.float32),
+        down.reshape(8, 1152, 128).transpose(1, 0, 2).reshape(1152, 1024).astype(jnp.float32),
     )
 
 

time: 1600 us -> 253 us (0.16)
  waiting for transfers between devices: 761 us -> 0 us
  blocking collectives: 681 us -> 0 us
  Pallas kernels: 0 us -> 165 us
  local copies, waits for them, and re-layouts: 44.7 us -> 22.4 us
  between operations: 18 us -> 1.62 us
    reduce_scatter x7 -> x0, waiting for transfers between devices: 563 us -> none  [the longest x1 228 us: body(): lax.psum_scatter(mlp_sums[2].astype(jnp.bfloat16), 'dp', scatter_dimensio...]
    all_gather x6 -> x0, blocking collectives: 375 us -> none  [the longest x1 91.7 us: body(): lax.all_gather(every_part[1].astype(jnp.bfloat16), 'dp', axis=0, tiled=True)]
    unnamed x3 -> x0, blocking collectives: 299 us -> none
    pallas_call x0 -> x5, Pallas kernels: none -> 165 us  [the longest x1 124 us: all_reduce(): pl.pallas_call(functools.partial(reduce_kernel, n, steps), out_shape=[jax...]
    all_gather x3 -> x0, waiting for transfers between devices: 113 us -> none  [the longest x1 67.6 us: body(): lax.all_gather(every_part[9].astype(jnp.bfloat16), 'dp', axis=0, tiled=True)]
    psum x3 -> x0, waiting for transfers between devices: 84.6 us -> none  [the longest x1 33 us: body(): lax.psum(d_one_part.astype(jnp.bfloat16), 'tensor').astype(jnp.float32)]
  transfers between devices with their start and end apart: 17 -> 0, of which waited for: 12 -> 0; matrix products, arithmetic and copies ran while one was open for 13% -> 0% of each run, Pallas kernels for 0% -> 0%
where the time goes in v1:
time: 253 us; the launch traced here: 252 us
  Pallas kernels  165 us (65%)
  other arithmetic  31.8 us (13%)
  matrix products  31.2 us (12%)
  local copies, waits for them, and re-layouts  22.4 us (9%)
    pallas_call x1, Pallas kernels, all_reduce(): pl.pallas_call(functools.partial(reduce_kernel, n, steps), out_shape=[jax...  124 us
    pallas_call x3, Pallas kernels, tensor_sums(): pl.pallas_call(functools.partial(sums_kernel, kinds), out_shape=out_shape...  32.2 us
    pallas_call x1, Pallas kernels, gather_pair(): pl.pallas_call(gather_kernel, out_shape=[shape, shape], in_specs=[V, V],...  9.18 us
    dot_general x7, matrix products, dot_last(): lax.dot_general(left_side, right_side, (((1,), (1,)), ((), ())), preferre...  8.51 us
    dot_general x7, matrix products, dot_rows(): lax.dot_general(left_side, right_side, (((0,), (0,)), ((), ())), preferre...  8.08 us
    convert_element_type x1, other arithmetic, body(): up.reshape(1024, 1152).astype(jnp.float32)  6.87 us
    unnamed x127, local copies, waits for them, and re-layouts  5.97 us

profile of v1, /device:TPU:0, one launch (start us, length us, event | category | flops | bytes accessed | tf_op | source)
XLA Modules:
  0.0 251.9 jit_solution(17952196233059163348)
XLA Ops:
  0.7 9.2 %gather_pair.1 = (bf16[144,1024]{1,0:T(8,128)(2,1)}, bf16[144,1024]{1,0:T(8,128)(2,1)}) custom-call(bf16[144,256]{1,0:T(8,128)(2,1)} %a.1, bf16[144,256]{1,0:T(8,128)(2,1)} %b.1), custom_call_target="tpu_custom_call" | custom-call | tf_op jit(solution)/shard_map/gather_pair/pallas_call | solution.py:319
  11.0 1.4 convolution_convert_fusion.9
  13.2 1.4 fusion.27
  18.2 1.8 subtract_convert_fusion
  20.1 1.7 copy.166
  28.4 2.1 fusion.34.refs_0_
  30.6 10.4 %tensor_sums.3 = bf16[144,1024]{1,0:T(8,128)(2,1)} custom-call(f32[144,1024]{1,0:T(8,128)} %fusion.34.refs_0_), custom_call_target="tpu_custom_call" | custom-call | tf_op jit(solution)/shard_map/tensor_sums/pallas_call | solution.py:411
  41.0 1.3 multiply_reduce_fusion.2
  43.9 2.2 fusion.36
  49.7 1.7 convolution_add_fusion.2.refs_0_
  51.4 1.4 fusion.38.refs_1_
  52.8 11.4 %tensor_sums.4 = (bf16[144,1024]{1,0:T(8,128)(2,1)}, f32[144,256]{1,0:T(8,128)}) custom-call(f32[144,1024]{1,0:T(8,128)} %convolution_add_fusion.2.refs_0_, f32[144,1024]{1,0:T(8,128)} %fusion.38.refs_1_), custom_call_target="tpu_custom_call" | custom-call | tf_op jit(solution)/shard_map/tensor_sums/pallas_call | solution.py:411
  64.2 1.9 fusion.10
  66.2 2.1 convert_bitcast_fusion.1
  70.2 1.5 copy.174
  74.6 1.4 fusion.39
  80.6 2.1 convolution_add_fusion.refs_0_
  83.7 10.4 %tensor_sums.5 = (bf16[144,1024]{1,0:T(8,128)(2,1)}, f32[8,128]{1,0:T(8,128)}) custom-call(f32[144,1024]{1,0:T(8,128)} %convolution_add_fusion.refs_0_, f32[8,128]{1,0:T(8,128)} %pad.4.refs_1_), custom_call_target="tpu_custom_call" | custom-call | tf_op jit(solution)/shard_map/tensor_sums/pallas_call | solution.py:411
  94.1 2.0 fusion.11
  96.1 1.7 fusion.17
  97.8 1.9 convolution_convert_fusion.2
  99.7 2.5 copy.181
  102.2 2.3 convolution_convert_fusion.1
  104.6 2.3 convolution_convert_fusion
  108.9 1.4 pad_maximum_fusion.refs_3_
  110.9 123.6 %dp_sum.1 = (bf16[2,4,4,288,128]{4,3,2,1,0:T(8,128)(2,1)}, bf16[2,4,4,32,1152]{4,3,2,1,0:T(8,128)(2,1)}, bf16[2,4,4,32,1152]{4,3,2,1,0:T(8,128)(2,1)}, bf16[2,4,4,32,768]{4,3,2,1,0:T(8,128)(2,1)}, f32[24,128]{1,0:T(8,128)}) custom-call(bf16[2,4,4,288,128]{4,3,2,1,0:T(8,128)(2,1)} %bitcast.142, bf16[2,4,4,32,1152]{4,3,2,1,0:T(8,128)(2,1)} %bitcast.143, ...), custom_call_target="tpu_custom_call" | custom-call | tf_op jit(solution)/shard_map/dp_sum/pallas_call | solution.py:260
  234.5 1.3 slice_bitcast_fusion
  235.8 1.6 bitcast_convert_fusion.2
  239.6 1.3 slice_bitcast_fusion.2
  240.9 1.3 copy.210
  242.2 6.9 %bitcast_convert_fusion = (f32[1024,1152]{1,0:T(8,128)}, f32[1024,1152]{1,0:T(8,128)}) fusion(bf16[2,4,4,32,1152]{4,3,2,1,0:T(8,128)(2,1)} %get-tuple-element.33, bf16[2,4,4,32,1152]{4,3,2,1,0:T(8,128)(2,1)} %get-tuple-element.32), kind=kLoop, calls=%fused_computation.5 | loop fusion | flops 2359296 | bytes 14155776 | tf_op jit(solution)/shard_map/convert_element_type | solution.py:654
  249.1 2.8 %copy_bitcast_fusion = f32[1152,1024]{1,0:T(8,128)} fusion(bf16[8,1152,128]{2,1,0:T(8,128)(2,1)S(1)} %bitcast.146), kind=kLoop, calls=%fused_computation | loop fusion | flops 1179648 | bytes 7077888 | tf_op jit(solution)/shard_map/convert_element_type | solution.py:655
  (211 shorter events, 32.0 us)
Async XLA Ops:
  0.6 46.4 %copy-start = (bf16[1024,1152]{1,0:T(8,128)(2,1)S(1)}, bf16[1024,1152]{1,0:T(8,128)(2,1)}, u32[]{:S(2)}) copy-start(bf16[1024,1152]{1,0:T(8,128)(2,1)} %param.25) | copy-start | bytes 7077892
  0.7 15.3 %copy-start.54 = (f32[64]{0:T(128)S(1)}, f32[64]{0:T(128)}, u32[]{:S(2)}) copy-start(f32[64]{0:T(128)} %param.20) | copy-start | bytes 772
  0.7 15.5 %copy-start.61 = (s32[1,4]{1,0:T(1,128)S(1)}, s32[1,4]{1,0:T(1,128)}, u32[]{:S(2)}) copy-start(s32[1,4]{1,0:T(1,128)} %param.15) | copy-start | bytes 52
  11.0 11.5 %copy-start.52 = (f32[144]{0:T(256)}, f32[144]{0:T(256)S(1)}, u32[]{:S(2)}) copy-start(f32[144]{0:T(256)S(1)} %add_rsqrt_fusion.3) | copy-start | bytes 1732
  12.3 10.1 %copy-start.2 = (bf16[144,1024]{1,0:T(8,128)(2,1)S(1)}, bf16[144,1024]{1,0:T(8,128)(2,1)}, u32[]{:S(2)}) copy-start(bf16[144,1024]{1,0:T(8,128)(2,1)} %get-tuple-element.24) | copy-start | bytes 884740
  12.4 10.1 %copy-start.56 = (f32[1024]{0:T(1024)S(1)}, f32[1024]{0:T(1024)}, u32[]{:S(2)}) copy-start(f32[1024]{0:T(1024)} %param.16) | copy-start | bytes 12292
  14.8 10.2 %copy-start.6 = (f32[144,4,64]{2,1,0:T(4,128)}, f32[144,4,64]{2,1,0:T(4,128)S(1)}, u32[]{:S(2)}) copy-start(f32[144,4,64]{2,1,0:T(4,128)S(1)} %reshape.318) | copy-start | bytes 442372
  14.8 10.1 %copy-start.59 = (f32[64]{0:T(128)S(1)}, f32[64]{0:T(128)}, u32[]{:S(2)}) copy-start(f32[64]{0:T(128)} %param.21) | copy-start | bytes 772
  17.4 9.2 %copy-start.34 = (f32[144,32]{0,1:T(8,128)}, f32[144,32]{0,1:T(8,128)S(1)}, u32[]{:S(2)}) copy-start(f32[144,32]{0,1:T(8,128)S(1)} %get-tuple-element.76) | copy-start | bytes 55300
  18.2 8.5 %copy-start.26 = (f32[144,32]{1,0:T(8,128)}, f32[144,32]{1,0:T(8,128)S(1)}, u32[]{:S(2)}) copy-start(f32[144,32]{1,0:T(8,128)S(1)} %copy.163) | copy-start | bytes 55300
  25.1 5.5 %copy-start.44 = (bf16[144,2,32]{0,2,1:T(8,128)(2,1)}, bf16[144,2,32]{0,2,1:T(8,128)(2,1)S(1)}, u32[]{:S(2)}) copy-start(bf16[144,2,32]{0,2,1:T(8,128)(2,1)S(1)} %get-tuple-element.66) | copy-start | bytes 55300
  25.1 5.5 %copy-start.46 = (bf16[144,2,32]{0,2,1:T(8,128)(2,1)}, bf16[144,2,32]{0,2,1:T(8,128)(2,1)S(1)}, u32[]{:S(2)}) copy-start(bf16[144,2,32]{0,2,1:T(8,128)(2,1)S(1)} %get-tuple-element.67) | copy-start | bytes 55300
  26.7 16.1 %copy-start.48 = (f32[1024]{0:T(1024)S(1)}, f32[1024]{0:T(1024)}, u32[]{:S(2)}) copy-start(f32[1024]{0:T(1024)} %param.23) | copy-start | bytes 12292
  40.9 5.2 %copy-start.4 = (bf16[1152,1024]{1,0:T(8,128)(2,1)S(1)}, bf16[1152,1024]{1,0:T(8,128)(2,1)}, u32[]{:S(2)}) copy-start(bf16[1152,1024]{1,0:T(8,128)(2,1)} %param.26) | copy-start | bytes 7077892
  41.0 5.2 %copy-start.8 = (bf16[144,1024]{1,0:T(8,128)(2,1)S(1)}, bf16[144,1024]{1,0:T(8,128)(2,1)}, u32[]{:S(2)}) copy-start(bf16[144,1024]{1,0:T(8,128)(2,1)} %get-tuple-element.25) | copy-start | bytes 884740
  51.4 12.8 %copy-start.5 = (bf16[144,1024]{1,0:T(8,128)(2,1)S(1)}, bf16[144,1024]{1,0:T(8,128)(2,1)}, u32[]{:S(2)}) copy-start(bf16[144,1024]{1,0:T(8,128)(2,1)} %tensor_sums.3) | copy-start | bytes 884740
  51.4 12.8 %copy-start.51 = (f32[144]{0:T(256)S(1)}, f32[144]{0:T(256)}, u32[]{:S(2)}) copy-start(f32[144]{0:T(256)} %copy-done.50) | copy-start | bytes 1732
  51.4 14.8 %copy-start.9 = (bf16[144,1024]{1,0:T(8,128)(2,1)S(1)}, bf16[144,1024]{1,0:T(8,128)(2,1)}, u32[]{:S(2)}) copy-start(bf16[144,1024]{1,0:T(8,128)(2,1)} %get-tuple-element.25) | copy-start | bytes 884740
  52.8 15.5 %copy-start.12 = (bf16[256,1024]{1,0:T(8,128)(2,1)S(1)}, bf16[256,1024]{1,0:T(8,128)(2,1)}, u32[]{:S(2)}) copy-start(bf16[256,1024]{1,0:T(8,128)(2,1)} %param.22) | copy-start | bytes 1572868
  64.2 4.6 %copy-start.40 = (bf16[144,2,64,1]{0,2,3,1:T(8,128)(2,1)S(1)}, bf16[144,2,64,1]{0,2,3,1:T(8,128)(2,1)}, u32[]{:S(2)}) copy-start(bf16[144,2,64,1]{0,2,3,1:T(8,128)(2,1)} %copy.189) | copy-start | bytes 110596
  73.3 3.8 %copy-start.35 = (f32[144,32]{0,1:T(8,128)S(1)}, f32[144,32]{0,1:T(8,128)}, u32[]{:S(2)}) copy-start(f32[144,32]{0,1:T(8,128)} %copy-done.34) | copy-start | bytes 55300
  73.4 3.8 %copy-start.38 = (f32[144,32]{0,1:T(8,128)S(1)}, f32[144,32]{0,1:T(8,128)}, u32[]{:S(2)}) copy-start(f32[144,32]{0,1:T(8,128)} %get-tuple-element.74) | copy-start | bytes 55300
  74.6 4.4 %copy-start.36 = (bf16[144,256]{1,0:T(8,128)(2,1)}, bf16[144,256]{1,0:T(8,128)(2,1)S(1)}, u32[]{:S(2)}) copy-start(bf16[144,256]{1,0:T(8,128)(2,1)S(1)} %get-tuple-element.54) | copy-start | bytes 221188
  76.0 4.3 %copy-start.25 = (bf16[144,256]{0,1:T(8,128)(2,1)S(1)}, bf16[144,256]{0,1:T(8,128)(2,1)}, u32[]{:S(2)}) copy-start(bf16[144,256]{0,1:T(8,128)(2,1)} %copy-done.24) | copy-start | bytes 221188
  78.1 16.0 %copy-start.53 = (f32[144]{0:T(256)S(1)}, f32[144]{0:T(256)}, u32[]{:S(2)}) copy-start(f32[144]{0:T(256)} %copy-done.52) | copy-start | bytes 1732
  78.1 16.0 %copy-start.57 = (f32[1024]{0:T(1024)S(1)}, f32[1024]{0:T(1024)}, u32[]{:S(2)}) copy-start(f32[1024]{0:T(1024)} %param.16) | copy-start | bytes 12292
  79.1 15.0 %copy-start.41 = (bf16[144,128]{1,0:T(8,128)(2,1)}, bf16[144,128]{1,0:T(8,128)(2,1)S(1)}, u32[]{:S(2)}) copy-start(bf16[144,128]{1,0:T(8,128)(2,1)S(1)} %get-tuple-element.63) | copy-start | bytes 110596
  80.5 17.2 %copy-start.30 = (bf16[2,64,144]{2,1,0:T(8,128)(2,1)}, bf16[2,64,144]{2,1,0:T(8,128)(2,1)S(1)}, u32[]{:S(2)}) copy-start(bf16[2,64,144]{2,1,0:T(8,128)(2,1)S(1)} %fusion.4) | copy-start | bytes 110596
  80.6 15.6 %copy-start.43 = (f32[144,256]{1,0:T(8,128)S(1)}, f32[144,256]{1,0:T(8,128)}, u32[]{:S(2)}) copy-start(f32[144,256]{1,0:T(8,128)} %get-tuple-element.26) | copy-start | bytes 442372
  80.6 17.2 %copy-start.10 = (bf16[144,1024]{1,0:T(8,128)(2,1)S(1)}, bf16[144,1024]{1,0:T(8,128)(2,1)}, u32[]{:S(2)}) copy-start(bf16[144,1024]{1,0:T(8,128)(2,1)} %get-tuple-element.25) | copy-start | bytes 884740
  102.2 4.6 %copy-start.18 = (bf16[1024,144]{0,1:T(8,128)(2,1)S(1)}, bf16[1024,144]{0,1:T(8,128)(2,1)}, u32[]{:S(2)}) copy-start(bf16[1024,144]{0,1:T(8,128)(2,1)} %get-tuple-element.39) | copy-start | bytes 884740
  242.2 6.9 %copy-start.11 = (bf16[2,4,4,288,128]{4,3,2,1,0:T(8,128)(2,1)S(1)}, bf16[2,4,4,288,128]{4,3,2,1,0:T(8,128)(2,1)}, u32[]{:S(2)}) copy-start(bf16[2,4,4,288,128]{4,3,2,1,0:T(8,128)(2,1)} %get-tuple-element.34) | copy-start | bytes 7077892
  (30 other events, 65.8 us)

commit v2 on v1

v2 whole, which is shorter than its diff:
```python
import functools
import jax
import jax.numpy as jnp
from jax import lax
from jax.experimental import pallas as pl
from jax.experimental.pallas import tpu as pltpu
from jax.sharding import PartitionSpec as P

HEAD_SIZE = 64
MESH = pl.DeviceIdType.MESH


def add_into(out, parts, step):
    lead = out.shape[0]
    rows = out.shape[1]
    per = rows // step

    def add_step(i, _):
        b = i // per
        r = pl.multiple_of((i % per) * step, 16)
        total = parts[0][b, pl.ds(r, step), :].astype(jnp.float32)
        for part in parts[1:]:
            total = total + part[b, pl.ds(r, step), :].astype(jnp.float32)
        out[b, pl.ds(r, step), :] = total.astype(jnp.bfloat16)
        return 0

    lax.fori_loop(0, lead * per, add_step, 0)


(T1P, T1M, I1P, I1M, M1P, M1M, T2P, T2M, I2P, I2M, M2P, M2M, Y, A2P, A2M, F2P, F2M, A1P, A1M, F1P, F1M) = range(21)
KEYS = 21


class Chunk:
    def __init__(self, src, dst, t1, r1, m1, s1, t2, r2, m2, s2, yb, send, recv, step, where):
        self.src, self.dst = src, dst
        self.t1, self.r1, self.m1, self.s1 = t1, r1, m1, s1
        self.t2, self.r2, self.m2, self.s2, self.yb = t2, r2, m2, s2, yb
        self.send, self.recv, self.step = send, recv, step
        y, z, x = where
        self.where = where

        def dev(yy, zz, xx):
            return {"dp": (yy * 4 + zz) * 4 + xx}

        up = lambda v: lax.rem(v + 1, 4)
        down = lambda v: lax.rem(v + 3, 4)
        xp, xm = dev(y, z, up(x)), dev(y, z, down(x))
        zp, zm = dev(y, up(z), x), dev(y, down(z), x)
        self.ynb = dev(1 - y, z, x)
        self.first = ((x, xp, xm), (z, zp, zm))
        self.second = ((z, zp, zm), (x, xp, xm))
        self.live = {}

    def go(self, h, name, src, dst, device):
        k = h * KEYS + name
        c = pltpu.make_async_remote_copy(
            src_ref=src, dst_ref=dst, send_sem=self.send.at[k], recv_sem=self.recv.at[k],
            device_id=device, device_id_type=MESH)
        c.start()
        self.live[h, name] = c

    def got(self, h, *names):
        for n in names:
            self.live[h, n].wait_recv()

    def start1(self):
        for h in range(2):
            p, plus, minus = self.first[h]
            k2, kp, km = lax.rem(p + 2, 4), lax.rem(p + 1, 4), lax.rem(p + 3, 4)
            H, T, R = self.src.at[h], self.t1.at[h], self.r1.at[h]
            self.go(h, T1P, H.at[k2, pl.ds(0, 2)], T.at[0], plus)
            self.go(h, T1M, H.at[k2, pl.ds(2, 2)], T.at[1], minus)
            self.go(h, I1P, H.at[kp, pl.ds(2, 2)], R.at[0, pl.ds(2, 2)], plus)
            self.go(h, I1M, H.at[km, pl.ds(0, 2)], R.at[1, pl.ds(0, 2)], minus)

    def mid1(self):
        for h in range(2):
            p, plus, minus = self.first[h]
            kp, km = lax.rem(p + 1, 4), lax.rem(p + 3, 4)
            H, T, R, M = self.src.at[h], self.t1.at[h], self.r1.at[h], self.m1.at[h]
            self.got(h, T1P)
            add_into(M.at[0], (H.at[kp, pl.ds(0, 2)], T.at[0]), self.step)
            self.go(h, M1P, M.at[0], R.at[0, pl.ds(0, 2)], plus)
            self.got(h, T1M)
            add_into(M.at[1], (H.at[km, pl.ds(2, 2)], T.at[1]), self.step)
            self.go(h, M1M, M.at[1], R.at[1, pl.ds(2, 2)], minus)

    def fin1(self):
        for h in range(2):
            p = self.first[h][0]
            R = self.r1.at[h]
            self.got(h, I1P, I1M, M1P, M1M)
            add_into(self.s1.at[h], (self.src.at[h, p], R.at[0], R.at[1]), self.step)
            p, plus, minus = self.second[h]
            k2, kp, km = lax.rem(p + 2, 4), lax.rem(p + 1, 4), lax.rem(p + 3, 4)
            H, T, R = self.s1.at[h], self.t2.at[h], self.r2.at[h]
            half = T.shape[1]
            lo, hi = pl.ds(0, half), pl.ds(half, half)
            self.go(h, T2P, H.at[k2, lo], T.at[0], plus)
            self.go(h, T2M, H.at[k2, hi], T.at[1], minus)
            self.go(h, I2P, H.at[kp, hi], R.at[0, hi], plus)
            self.go(h, I2M, H.at[km, lo], R.at[1, lo], minus)

    def mid2(self):
        for h in range(2):
            p, plus, minus = self.second[h]
            kp, km = lax.rem(p + 1, 4), lax.rem(p + 3, 4)
            H, T, R, M = self.s1.at[h], self.t2.at[h], self.r2.at[h], self.m2.at[h]
            half = T.shape[1]
            lo, hi = pl.ds(0, half), pl.ds(half, half)
            step = min(self.step, half)
            self.got(h, T2P)
            add_into(M.at[pl.ds(0, 1)], (H.at[pl.ds(kp, 1), lo], T.at[pl.ds(0, 1)]), step)
            self.go(h, M2P, M.at[0], R.at[0, lo], plus)
            self.got(h, T2M)
            add_into(M.at[pl.ds(1, 1)], (H.at[pl.ds(km, 1), hi], T.at[pl.ds(1, 1)]), step)
            self.go(h, M2M, M.at[1], R.at[1, hi], minus)

    def fin2(self):
        for h in range(2):
            p = self.second[h][0]
            R = self.r2.at[h]
            self.got(h, I2P, I2M, M2P, M2M)
            add_into(self.s2.at[pl.ds(h, 1)], (self.s1.at[h, pl.ds(p, 1)], R.at[pl.ds(0, 1)], R.at[pl.ds(1, 1)]), self.step)
            self.go(h, Y, self.s2.at[h], self.yb.at[h], self.ynb)

    def finy(self):
        for h in range(2):
            a = self.first[h][0]
            p, plus, minus = self.second[h]
            self.got(h, Y)
            add_into(self.dst.at[h, a, pl.ds(p, 1)], (self.s2.at[pl.ds(h, 1)], self.yb.at[pl.ds(h, 1)]), self.step)
            blk = self.dst.at[h, a, p]
            self.go(h, A2P, blk, blk, plus)
            self.go(h, A2M, blk, blk, minus)

    def ag2(self):
        for h in range(2):
            a = self.first[h][0]
            p, plus, minus = self.second[h]
            kp, km = lax.rem(p + 1, 4), lax.rem(p + 3, 4)
            half = self.t2.shape[2]
            self.got(h, A2P)
            blk = self.dst.at[h, a, km, pl.ds(0, half)]
            self.go(h, F2P, blk, blk, plus)
            self.got(h, A2M)
            blk = self.dst.at[h, a, kp, pl.ds(half, half)]
            self.go(h, F2M, blk, blk, minus)

    def ag1s(self):
        for h in range(2):
            p, plus, minus = self.first[h]
            self.got(h, F2P, F2M)
            blk = self.dst.at[h, p]
            self.go(h, A1P, blk, blk, plus)
            self.go(h, A1M, blk, blk, minus)

    def ag1(self):
        for h in range(2):
            p, plus, minus = self.first[h]
            kp, km = lax.rem(p + 1, 4), lax.rem(p + 3, 4)
            self.got(h, A1P)
            blk = self.dst.at[h, km, pl.ds(0, 2)]
            self.go(h, F1P, blk, blk, plus)
            self.got(h, A1M)
            blk = self.dst.at[h, kp, pl.ds(2, 2)]
            self.go(h, F1M, blk, blk, minus)

    def end(self):
        for h in range(2):
            self.got(h, F1P, F1M)
        for c in self.live.values():
            c.wait_send()

    def stages(self):
        return [self.start1, self.mid1, self.fin1, self.mid2, self.fin2, self.finy, self.ag2, self.ag1s, self.ag1, self.end]


def coords():
    d = lax.axis_index("dp")
    return d // 16, (d // 4) % 4, d % 4


def scratch_for(shape):
    _, _, _, R, C = shape
    bf = jnp.bfloat16
    return [
        pltpu.VMEM((2, 2, 2, R, C), bf), pltpu.VMEM((2, 2, 4, R, C), bf), pltpu.VMEM((2, 2, 2, R, C), bf), pltpu.VMEM((2, 4, R, C), bf),
        pltpu.VMEM((2, 2, R // 2, C), bf), pltpu.VMEM((2, 2, R, C), bf), pltpu.VMEM((2, 2, R // 2, C), bf), pltpu.VMEM((2, R, C), bf), pltpu.VMEM((2, R, C), bf),
        pltpu.SemaphoreType.DMA((2 * KEYS,)), pltpu.SemaphoreType.DMA((2 * KEYS,)),
    ]

NS = 11

def tensor_place():
    t = lax.axis_index("tensor")
    core, side = lax.rem(t, 2), t // 2
    return side, core, side * 2 + (1 - core), (1 - side) * 2 + core


def send(src, dst, sems, k, peer):
    c = pltpu.make_async_remote_copy(
        src_ref=src, dst_ref=dst, send_sem=sems[0].at[k], recv_sem=sems[1].at[k],
        device_id={"tensor": peer}, device_id_type=MESH)
    c.start()
    return c


def greet(sib, far):
    barrier = pltpu.get_barrier_semaphore()
    for peer in (sib, far):
        pl.semaphore_signal(barrier, inc=1, device_id={"tensor": peer}, device_id_type=MESH)
    pl.semaphore_wait(barrier, 2)


def columns(block):
    return pl.ds(pl.multiple_of(block * 256, 256), 256)


def sum_steps(part, out, low, near, mid, away, sems, base, place, scatter):
    side, core, sib, far = place
    live = []

    def one():
        low[...] = part[...].astype(jnp.bfloat16)
        for s in range(2):
            live.append(send(low.at[:, columns(s * 2 + 1 - core)], near.at[s], sems, base + s, sib))

    def two():
        order = (1 - side, side)
        for s in range(2):
            live[s].wait_recv()
        for i, s in enumerate(order):
            mid[s] = (low[:, columns(s * 2 + core)].astype(jnp.float32) + near[s].astype(jnp.float32)).astype(jnp.bfloat16)
            if i == 0 or not scatter:
                live.append(send(mid.at[s], away.at[s], sems, base + 2 + i, far))

    def three():
        if scatter:
            live[2].wait_recv()
            out[...] = mid[side].astype(jnp.float32) + away[side].astype(jnp.float32)
            return
        for i, s in enumerate((1 - side, side)):
            live[2 + i].wait_recv()
        for i, s in enumerate((1 - side, side)):
            there = out.at[:, columns(s * 2 + core)]
            out[:, columns(s * 2 + core)] = (mid[s].astype(jnp.float32) + away[s].astype(jnp.float32)).astype(jnp.bfloat16)
            live.append(send(there, there, sems, base + 4 + i, sib))

    def four():
        for c in live[4:]:
            c.wait_recv()
        for c in live:
            c.wait_send()

    return [one, two, three, four]


class SmallSum:
    def __init__(self, where, vec, out, slots, mine, send_sem, recv_sem):
        y, z, x = where
        self.vec, self.out, self.slots, self.mine = vec, out, slots, mine
        self.sems = (send_sem, recv_sem)
        self.axes = (
            (x, 4, lambda v: (y * 4 + z) * 4 + v),
            (z, 4, lambda v: (y * 4 + v) * 4 + x),
            (y, 2, lambda v: (v * 4 + z) * 4 + x),
        )
        self.live = []

    def begin(self, s, value):
        p, n, dev = self.axes[s]
        self.mine[s] = value
        self.slots[s, p] = value
        self.live = []
        for i in range(1, n):
            k = s * 3 + i - 1
            c = pltpu.make_async_remote_copy(
                src_ref=self.mine.at[s], dst_ref=self.slots.at[s, p], send_sem=self.sems[0].at[k], recv_sem=self.sems[1].at[k],
                device_id={"dp": dev(lax.rem(p + i, n))}, device_id_type=MESH)
            c.start()
            self.live.append(c)

    def close(self, s):
        for c in self.live:
            c.wait()
        value = self.slots[s, 0]
        for i in range(1, self.axes[s][1]):
            value = value + self.slots[s, i]
        return value

    def one(self):
        self.begin(0, self.vec[...])

    def two(self):
        self.begin(1, self.close(0))

    def three(self):
        self.begin(2, self.close(1))

    def four(self):
        self.out[...] = self.close(2)


def small_steps(v, out, near, mid, away, sems, base, place):
    side, core, sib, far = place
    live = []

    def one():
        live.append(send(v, near, sems, base, sib))

    def two():
        live[0].wait()
        mid[...] = v[...] + near[...]
        live.append(send(mid, away, sems, base + 1, far))

    def three():
        live[1].wait()
        out[...] = mid[...] + away[...]

    return [one, two, three]


def swap_halves(v):
    n = v.shape[1]
    lane = lax.broadcasted_iota(jnp.int32, v.shape, 1) % 64
    return jnp.where(lane < 32, pltpu.roll(v, n - 32, 1), pltpu.roll(v, 32, 1))


def head_means(v, heads):
    return [jnp.mean(v[:, 64 * h:64 * h + 64], axis=-1, keepdims=True) for h in range(heads)]


def spread(cols, heads):
    return jnp.concatenate([jnp.broadcast_to(c, (c.shape[0], 64)) for c in cols], axis=1)


CHUNK_SHAPES = ((2, 4, 4, 32, 1152),) * 3 + ((2, 4, 4, 32, 768),)


def big_kernel(*refs):
    (
        r_tokens, r_cotangent, r_lengths, r_frequency, r_attn_gain, r_mlp_gain, r_q_gain, r_k_gain,
        r_w_query, r_w_key, r_w_value, r_w_output, h_gate, h_up, h_down,
    ) = refs[:15]
    h_sums, (r_vec_sum, r_block_out, r_input_grad) = refs[15:19], refs[19:22]
    rest = refs[22:]
    groups = [rest[NS * c:NS * c + NS] for c in range(4)]
    rest = rest[NS * 4:]
    small_refs, grads, sums, rest = rest[:4], rest[4:8], rest[8:12], rest[12:]
    (r_vec, r_d_two, r_own, r_d_one, r_gains, r_gains_sum, r_part, r_d_hidden, r_d_low, r_d_qkv) = rest[:10]
    (r_x, r_cot, r_normed_one, r_normed_two, r_attended, r_hidden, r_d_two_part, r_mlp_part) = rest[10:18]
    (r_q_low, r_k_low, r_v_low, r_q_plain, r_k_plain, r_q_inv, r_k_inv, r_cosine, r_sine, r_p, r_heads_out) = rest[18:29]
    (r_act, r_d_gate, r_d_up, w_gate, w_up, w_down) = rest[29:35]
    rest = rest[35:]
    ts, tb, tc, ta, td = rest[:4], rest[4:8], rest[8:12], rest[12:16], rest[16:19]
    sems, load_sem, store_sem = rest[19:21], rest[21], rest[22]
    where, place = coords(), tensor_place()
    side, core, sib, far = place
    me = side * 2 + core
    y, z, x = where
    f32, bf = jnp.float32, jnp.bfloat16
    loads = []
    for k, (there, here) in enumerate(((h_gate, w_gate), (h_up, w_up), (h_down, w_down))):
        loads.append(pltpu.make_async_copy(there, here, load_sem.at[k]))
        loads[k].start()
    barrier = pltpu.get_barrier_semaphore()
    peers = [(y, z, lax.rem(x + k, 4)) for k in (1, 2, 3)] + [(y, lax.rem(z + k, 4), x) for k in (1, 2, 3)] + [(1 - y, z, x)]
    for a, b, c in peers:
        pl.semaphore_signal(barrier, inc=1, device_id={"dp": (a * 4 + b) * 4 + c}, device_id_type=MESH)
    for peer in (sib, far):
        pl.semaphore_signal(barrier, inc=1, device_id={"tensor": peer}, device_id_type=MESH)
    pl.semaphore_wait(barrier, len(peers) + 2)

    c0, c1, c2, c3 = [Chunk(grads[c], sums[c], *groups[c], 16, where) for c in range(4)]
    r_attn = grads[3]
    small = SmallSum(where, r_vec, r_vec_sum, *small_refs)
    attended = sum_steps(r_part, r_attended, *ts, sems, 0, place, False)
    two = sum_steps(r_d_two_part, r_d_two, *ta, sems, 6, place, False)
    own = sum_steps(r_mlp_part, r_own, *tb, sems, 12, place, True)
    one = sum_steps(r_part, r_d_one, *tc, sems, 18, place, False)
    gains = small_steps(r_gains, r_gains_sum, *td, sems, 24, place)
    rows = r_x.shape[0]
    stores = []

    def leave(c, chunk):
        def finish():
            chunk.end()
            out = pltpu.make_async_copy(sums[c], h_sums[c], store_sem.at[c])
            out.start()
            stores.append(out)

        return finish

    def row_blocks(step, start):
        return lax.fori_loop(0, rows // 16, lambda b, v: step(pl.ds(pl.multiple_of(b * 16, 16), 16), v), start)

    pairs = ((r_tokens, r_x), (r_cotangent, r_cot))
    moves = {}

    def gather_start():
        for k, (v, o) in enumerate(pairs):
            there = o.at[:, columns(me)]
            moves[k] = (send(v, there, sems, 26 + 3 * k, far), send(v, there, sems, 27 + 3 * k, sib))
        for v, o in pairs:
            o[:, columns(me)] = v[...]

    def gather_pass(k):
        moves[k][0].wait_recv()
        there = pairs[k][1].at[:, columns(far)]
        moves[k + 2] = (send(there, there, sems, 28 + 3 * k, sib),)

    def gather_end(k):
        moves[k][0].wait_send()
        moves[k][1].wait()
        moves[k + 2][0].wait()

    def tables():
        lengths = r_lengths[...]
        one_length = [lengths[:, k:k + 1] for k in range(4)]
        ends = [one_length[0]]
        for k in range(1, 4):
            ends.append(ends[-1] + one_length[k])

        def segment(row):
            total = jnp.zeros(row.shape, jnp.int32)
            for end in ends:
                total = total + jnp.where(row >= end, 1, 0)
            return total

        row = lax.broadcasted_iota(jnp.int32, (rows, 128), 0)
        start = jnp.zeros(row.shape, jnp.int32)
        for end, length in zip(ends, one_length):
            start = start + jnp.where(row >= end, length, 0)
        angles = (row - start).astype(f32) * r_frequency[...]
        lane = lax.broadcasted_iota(jnp.int32, (rows, 128), 1) % 64
        cosine, sine = jnp.cos(angles), jnp.sin(angles)
        sine = jnp.where(lane < 32, -sine, sine)
        for k in (0, 128):
            r_cosine[:, k:k + 128] = cosine
            r_sine[:, k:k + 128] = sine
        query_row = lax.broadcasted_iota(jnp.int32, (rows, rows), 0)
        key_row = lax.broadcasted_iota(jnp.int32, (rows, rows), 1)
        moves[9] = (segment(query_row) == segment(key_row)) & (query_row >= key_row)

    def attn_norm():
        gain = r_attn_gain[...]

        def block(at, v):
            resid = r_x[at, :].astype(f32)
            inverse = lax.rsqrt(jnp.mean(resid * resid, axis=-1, keepdims=True) + EPS)
            r_normed_one[at, :] = (resid * inverse * gain).astype(bf)
            return v

        row_blocks(block, 0)

    def attention():
        normed = r_normed_one[...]
        r_v_low[...] = jnp.dot(normed, r_w_value[...], preferred_element_type=f32).astype(bf)
        for weight, gain, low, plain_ref, inv_ref, heads in (
            (r_w_query, r_q_gain, r_q_low, r_q_plain, r_q_inv, 4), (r_w_key, r_k_gain, r_k_low, r_k_plain, r_k_inv, 2)):
            width = 64 * heads
            raw = jnp.dot(normed, weight[...], preferred_element_type=f32)
            inv = spread([lax.rsqrt(m + EPS) for m in head_means(raw * raw, heads)], heads)
            plain = raw * inv
            inv_ref[...] = inv
            plain_ref[...] = plain
            scaled = plain * gain[...]
            low[...] = (scaled * r_cosine[:, :width] + swap_halves(scaled) * r_sine[:, :width]).astype(bf)
        out = []
        for h in range(4):
            at = slice(64 * (h // 2), 64 * (h // 2) + 64)
            scores = dot_last(r_q_low[:, 64 * h:64 * h + 64], r_k_low[:, at]) * HEAD_SIZE ** (-0.5)
            scores = jnp.where(moves[9], scores, -1e30)
            weights = jnp.exp(scores - jnp.max(scores, axis=-1, keepdims=True))
            p = weights / jnp.sum(weights, axis=-1, keepdims=True)
            r_p[h] = p
            out.append(jnp.dot(p.astype(bf), r_v_low[:, at], preferred_element_type=f32))
        heads_out = jnp.concatenate(out, axis=1).astype(bf)
        r_heads_out[...] = heads_out
        r_part[...] = jnp.dot(heads_out, r_w_output[...], preferred_element_type=f32)

    def mlp_norm():
        gain = r_mlp_gain[...]

        def block(at, v):
            hidden = r_x[at, :].astype(f32) + r_attended[at, :].astype(f32)
            r_hidden[at, :] = hidden
            inverse = lax.rsqrt(jnp.mean(hidden * hidden, axis=-1, keepdims=True) + EPS)
            r_normed_two[at, :] = (hidden * inverse * gain).astype(bf)
            return v

        row_blocks(block, 0)

    def mlp_units():
        for load in loads:
            load.wait()

        def tile(j, v):
            at = pl.ds(pl.multiple_of(j * 384, 128), 384)
            gate = jnp.dot(r_normed_two[...], w_gate[:, at], preferred_element_type=f32)
            up = jnp.dot(r_normed_two[...], w_up[:, at], preferred_element_type=f32)
            s = jax.nn.sigmoid(gate)
            silu = gate * s
            r_act[:, at] = (silu * up).astype(bf)
            d_act = dot_last(r_cot[...], w_down[at, :])
            r_d_gate[:, at] = (d_act * up * s * (1.0 + gate * (1.0 - s))).astype(bf)
            r_d_up[:, at] = (d_act * silu).astype(bf)
            return v

        lax.fori_loop(0, 3, tile, 0)

    def weight_grad(left, right, out):
        def tile(j, v):
            part = dot_rows(left[:, columns(j)], right[...]).astype(bf)
            out[j // 2, pl.ds((j % 2) * 2, 2)] = part.reshape(2, 4, 32, right.shape[1])
            return v

        return lambda: lax.fori_loop(0, 4, tile, 0)

    down_grad = weight_grad(r_cot, r_act, grads[0])
    gate_grad = weight_grad(r_normed_two, r_d_gate, grads[1])
    up_grad = weight_grad(r_normed_two, r_d_up, grads[2])

    def mlp_back():
        def tile(j, v):
            at = columns(j)
            r_d_two_part[:, at] = dot_last(r_d_gate[...], w_gate[at, :]) + dot_last(r_d_up[...], w_up[at, :])
            return v

        lax.fori_loop(0, 4, tile, 0)

    def mlp_out():
        def tile(j, v):
            at = columns(j)
            r_mlp_part[:, at] = jnp.dot(r_act[...], w_down[:, at], preferred_element_type=f32)
            return v

        lax.fori_loop(0, 4, tile, 0)

    def back_mlp_norm():
        gain = r_mlp_gain[...]

        def block(b, total):
            at = pl.ds(pl.multiple_of(b * 16, 16), 16)
            hidden = r_hidden[at, :]
            inverse = lax.rsqrt(jnp.mean(hidden * hidden, axis=-1, keepdims=True) + EPS)
            plain = hidden * inverse
            d_two = r_d_two[at, :].astype(jnp.float32)
            u = d_two * gain
            d_hidden = r_cot[at, :].astype(jnp.float32) + inverse * (
                u - plain * jnp.mean(u * plain, axis=-1, keepdims=True))
            r_d_hidden[at, :] = d_hidden
            r_d_low[at, :] = d_hidden.astype(jnp.bfloat16)
            return total + jnp.sum(d_two * plain, axis=0, keepdims=True)

        total = lax.fori_loop(0, rows // 16, block, jnp.zeros((1, 1024), jnp.float32))
        r_vec[...] = jnp.zeros((8, 1024), jnp.float32)
        r_vec[1:2, :] = total
        mine = columns(me)
        r_block_out[...] = (r_hidden[:, mine] + r_own[...]).astype(jnp.bfloat16)

    hold = {}

    def back_output():
        d_low = r_d_low[...]
        hold[0] = dot_last(d_low, r_w_output[...]).astype(jnp.bfloat16)
        r_attn[:, :, :, :, 512:768] = dot_rows(d_low, r_heads_out[...]).astype(jnp.bfloat16).reshape(2, 4, 4, 32, 256)

    def back_scores():
        d_heads = hold[0]
        scale = HEAD_SIZE ** (-0.5)
        d_query, d_key, d_value = [], [], []
        for j in range(2):
            at = slice(64 * j, 64 * j + 64)
            key, value = r_k_low[:, at], r_v_low[:, at]
            dk, dv = 0.0, 0.0
            for h in (2 * j, 2 * j + 1):
                p = r_p[h]
                dh = d_heads[:, 64 * h:64 * h + 64]
                d_probs = dot_last(dh, value)
                ds = (p * (d_probs - jnp.sum(d_probs * p, axis=-1, keepdims=True))).astype(jnp.bfloat16)
                d_query.append(jnp.dot(ds, key, preferred_element_type=jnp.float32) * scale)
                dk = dk + dot_rows(ds, r_q_low[:, 64 * h:64 * h + 64])
                dv = dv + dot_rows(p.astype(jnp.bfloat16), dh)
            d_key.append(dk * scale)
            d_value.append(dv)
        r_d_qkv[:, 384:512] = jnp.concatenate(d_value, axis=1).astype(jnp.bfloat16)
        hold[1] = jnp.concatenate(d_query, axis=1)
        hold[2] = jnp.concatenate(d_key, axis=1)

    def back_head_norm():
        r_gains[...] = jnp.zeros((8, 128), jnp.float32)
        for d, plain_ref, gain_ref, inv_ref, heads, put, place_at in (
            (hold[1], r_q_plain, r_q_gain, r_q_inv, 4, 0, 0), (hold[2], r_k_plain, r_k_gain, r_k_inv, 2, 256, 64)):
            width = 64 * heads
            turned = d * r_cosine[:, :width] - swap_halves(d) * r_sine[:, :width]
            plain = plain_ref[...]
            sums = jnp.sum(turned * plain, axis=0, keepdims=True)
            total = sums[:, :64]
            for h in range(1, heads):
                total = total + sums[:, 64 * h:64 * h + 64]
            r_gains[0:1, place_at:place_at + 64] = total
            u = turned * gain_ref[...]
            inv = inv_ref[...]
            back = inv * (u - plain * spread(head_means(u * plain, heads), heads))
            r_d_qkv[:, put:put + width] = back.astype(jnp.bfloat16)

    def back_project():
        dq, dk, dv = r_d_qkv[:, :256], r_d_qkv[:, 256:384], r_d_qkv[:, 384:512]
        r_part[...] = (
            dot_last(dq, r_w_query[...]) + dot_last(dk, r_w_key[...]) + dot_last(dv, r_w_value[...]))

    def back_attn_weights():
        r_attn[:, :, :, :, 0:512] = dot_rows(r_normed_one[...], r_d_qkv[...]).astype(jnp.bfloat16).reshape(2, 4, 4, 32, 512)

    def back_attn_norm():
        gain = r_attn_gain[...]
        mine = columns(me)

        def block(b, total):
            at = pl.ds(pl.multiple_of(b * 16, 16), 16)
            resid = r_x[at, :].astype(jnp.float32)
            inverse = lax.rsqrt(jnp.mean(resid * resid, axis=-1, keepdims=True) + EPS)
            plain = resid * inverse
            d_one = r_d_one[at, :].astype(jnp.float32)
            u = d_one * gain
            r_d_hidden[at, :] = r_d_hidden[at, :] + inverse * (
                u - plain * jnp.mean(u * plain, axis=-1, keepdims=True))
            return total + jnp.sum(d_one * plain, axis=0, keepdims=True)

        total = lax.fori_loop(0, rows // 16, block, jnp.zeros((1, 1024), jnp.float32))
        r_vec[0:1, :] = total
        r_vec[2:3, 0:128] = r_gains_sum[0:1, :]
        r_input_grad[...] = r_d_hidden[:, mine].astype(jnp.bfloat16)

    for step in (
        gather_start, tables, lambda: gather_pass(0), lambda: gather_pass(1), lambda: gather_end(0),
        attn_norm, attention, attended[0], lambda: gather_end(1), attended[1], attended[2], attended[3],
        mlp_norm, mlp_units, down_grad, c0.start1, gate_grad, c1.start1, mlp_back, two[0], up_grad, two[1], c0.mid1, c2.start1,
        mlp_out, two[2], own[0], two[3], own[1], own[2], c0.fin1, own[3], back_mlp_norm,
        back_output, c1.mid1, back_scores, c0.mid2, back_head_norm, back_project,
        one[0], gains[0], back_attn_weights, c3.start1, c0.fin2, one[1], gains[1], c1.fin1, c2.mid1, one[2], gains[2], c0.finy, one[3],
        back_attn_norm, small.one, c1.mid2, c0.ag2, c2.fin1, c3.mid1, c1.fin2, small.two, c0.ag1s, c1.finy, c2.mid2, c3.fin1,
        c1.ag2, c2.fin2, c3.mid2, small.three, c1.ag1s, c2.finy, c3.fin2, c0.ag1, c2.ag2, c3.finy, c2.ag1s, c3.ag2, small.four,
        c3.ag1s, c1.ag1, leave(0, c0), c2.ag1, leave(1, c1), c3.ag1, leave(2, c2), leave(3, c3),
    ):
        step()
    for out in stores:
        out.wait()


def big(arrays):
    V, A = pl.BlockSpec(memory_space=pltpu.VMEM), pl.BlockSpec(memory_space=pl.ANY)
    f32, bf = jnp.float32, jnp.bfloat16
    S = jax.ShapeDtypeStruct
    out_shape = [S(s, bf) for s in CHUNK_SHAPES] + [S((8, 1024), f32), S((144, 256), bf), S((144, 256), bf)]
    B = lambda *shape: pltpu.VMEM(shape, bf)
    F = lambda *shape: pltpu.VMEM(shape, f32)
    D = lambda n: pltpu.SemaphoreType.DMA((n,))
    scratch = sum([scratch_for(s) for s in CHUNK_SHAPES], [])
    scratch += [F(3, 4, 8, 1024), F(3, 8, 1024), D(9), D(9)]
    scratch += [B(*s) for s in CHUNK_SHAPES] * 2
    scratch += [F(8, 1024), B(144, 1024), F(144, 256), B(144, 1024), F(8, 128), F(8, 128), F(144, 1024), F(144, 1024), B(144, 1024), B(144, 512)]
    scratch += [B(144, 1024), B(144, 1024), B(144, 1024), B(144, 1024), B(144, 1024), F(144, 1024), F(144, 1024), F(144, 1024)]
    scratch += [B(144, 256), B(144, 128), B(144, 128), F(144, 256), F(144, 128), F(144, 256), F(144, 128), F(144, 256), F(144, 256), F(4, 144, 144), B(144, 256)]
    scratch += [B(144, 1152), B(144, 1152), B(144, 1152), B(1024, 1152), B(1024, 1152), B(1152, 1024)]
    scratch += ([B(144, 1024)] + [B(2, 144, 256)] * 3) * 4 + [F(8, 128)] * 3
    scratch += [D(32), D(32), D(3), D(4)]
    return pl.pallas_call(
        big_kernel, out_shape=out_shape, in_specs=[V] * 12 + [A] * 3, out_specs=[A] * 4 + [V] * 3, scratch_shapes=scratch,
        compiler_params=pltpu.CompilerParams(collective_id=0, has_side_effects=True, vmem_limit_bytes=61 * 1024 * 1024),
        name="block",
    )(*arrays)


def widen_kernel(gate, up, down, attn, o_gate, o_up, o_down, o_q, o_k, o_v, o_out):
    o_gate[...] = gate[...].astype(jnp.float32)
    o_up[...] = up[...].astype(jnp.float32)
    o_down[...] = down[...].astype(jnp.float32).T
    wide = attn[...].astype(jnp.float32)
    o_q[...] = wide[:, :256]
    o_k[...] = wide[:, 256:384]
    o_v[...] = wide[:, 384:512]
    o_out[...] = wide[:, 512:768].T


def widen(gate, up, down, attn):
    S = lambda *s: jax.ShapeDtypeStruct(s, jnp.float32)
    row = lambda w: pl.BlockSpec((128, w), lambda b: (b, 0))
    col = lambda h: pl.BlockSpec((h, 128), lambda b: (0, b))
    return pl.pallas_call(
        widen_kernel, grid=(8,),
        in_specs=[row(1152), row(1152), row(1152), row(768)],
        out_specs=[row(1152), row(1152), col(1152), row(256), row(128), row(128), col(256)],
        out_shape=[S(1024, 1152), S(1024, 1152), S(1152, 1024), S(1024, 256), S(1024, 128), S(1024, 128), S(256, 1024)],
        compiler_params=pltpu.CompilerParams(vmem_limit_bytes=60 * 1024 * 1024),
        name="widen",
    )(gate, up, down, attn)


EPS = 1e-05
THETA = 1000000.0


def dot_rows(left_side, right_side):
    return lax.dot_general(
        left_side, right_side, (((0,), (0,)), ((), ())), preferred_element_type=jnp.float32
    )


def dot_last(left_side, right_side):
    return lax.dot_general(
        left_side, right_side, (((1,), (1,)), ((), ())), preferred_element_type=jnp.float32
    )


def body(
    tokens,
    lengths,
    attn_gain,
    w_query,
    key_weight,
    value_weight,
    query_gain,
    key_gain,
    w_output,
    mlp_gain,
    w_gate,
    w_up,
    w_down,
    cotangent,
):
    frequency = THETA ** (-jnp.arange(32, dtype=jnp.float32) * 2.0 / HEAD_SIZE)
    down, gate, up, attn, vec, block_out, input_grad = big(
        (
            tokens,
            cotangent,
            lengths,
            jnp.tile(frequency[None], (1, 4)),
            attn_gain[None],
            mlp_gain[None],
            jnp.tile(query_gain[None], (1, 4)),
            jnp.tile(key_gain[None], (1, 2)),
            w_query,
            key_weight,
            value_weight,
            w_output,
            w_gate,
            w_up,
            w_down,
        )
    )
    gate, up, down, w_q, w_k, w_v, w_o = widen(
        gate.reshape(1024, 1152), up.reshape(1024, 1152), down.reshape(1024, 1152), attn.reshape(1024, 768)
    )
    return (
        block_out,
        input_grad,
        vec[0],
        w_q,
        w_k,
        w_v,
        vec[2, :64],
        vec[2, 64:128],
        w_o,
        vec[1],
        gate,
        up,
        down,
    )


def solution(mesh):
    in_specs = (
        P("dp", "tensor"),
        P("dp", None),
        P(),
        P(None, "tensor"),
        P(None, "tensor"),
        P(None, "tensor"),
        P(),
        P(),
        P("tensor", None),
        P(),
        P(None, "tensor"),
        P(None, "tensor"),
        P("tensor", None),
        P("dp", "tensor"),
    )
    out_specs = (
        P("dp", "tensor"),
        P("dp", "tensor"),
        P(),
        P(None, "tensor"),
        P(None, "tensor"),
        P(None, "tensor"),
        P(),
        P(),
        P("tensor", None),
        P(),
        P(None, "tensor"),
        P(None, "tensor"),
        P("tensor", None),
    )
    return jax.shard_map(body, mesh=mesh, in_specs=in_specs, out_specs=out_specs, check_vma=False)
```

time: 253 us -> 152 us (0.60)
  other arithmetic: 31.8 us -> 0.01 us
  matrix products: 31.2 us -> 0 us
  Pallas kernels: 165 us -> 143 us
  local copies, waits for them, and re-layouts: 22.4 us -> 7.2 us
    dot_general x27 -> x0, matrix products: 31.2 us -> none  [the longest x7 8.51 us: dot_last(): lax.dot_general(left_side, right_side, (((1,), (1,)), ((), ())), preferre...]
    pallas_call x5 -> x2, Pallas kernels: 165 us -> 143 us  [the longest x1 133 us: big(): pl.pallas_call(big_kernel, out_shape=out_shape, in_specs=[V] * 12 + [A] *...]
    convert_element_type x7 -> x0, other arithmetic: 14.2 us -> none  [the longest x1 6.87 us: body(): up.reshape(1024, 1152).astype(jnp.float32)]
    reduce_sum x14 -> x0, other arithmetic: 8.79 us -> none  [the longest x1 1.97 us: body(): attn_gain_grad = jnp.sum(d_one * plain_one, axis=0)]
    reshape x8 -> x0, local copies, waits for them, and re-layouts: 5.11 us -> none  [the longest x1 2.49 us: body(): w_down_grad.reshape(1152, 8, 128).transpose(1, 0, 2)]
    unnamed x127 -> x6, local copies, waits for them, and re-layouts: 5.97 us -> 1.28 us
where the time goes in v2:
time: 152 us; the launch traced here: 151 us
  Pallas kernels  143 us (94%)
  local copies, waits for them, and re-layouts  7.2 us (5%)
    pallas_call x1, Pallas kernels, big(): pl.pallas_call(big_kernel, out_shape=out_shape, in_specs=[V] * 12 + [A] *...  133 us
    pallas_call x1, Pallas kernels, widen(): pl.pallas_call(widen_kernel, grid=(8,), in_specs=[row(1152), row(1152), r...  10.7 us

profile of v2, /device:TPU:0, one launch (start us, length us, event | category | flops | bytes accessed | tf_op | source)
XLA Modules:
  0.0 151.1 jit_solution(18047280602067516642)
XLA Ops:
  0.7 0.7 tile.28
  1.3 0.6 tile.29.refs_7_
  1.9 0.6 tile.25.refs_3_
  2.5 0.7 tile.26
  3.2 0.6 tile.27.refs_6_
  3.8 132.6 %block.1 = (bf16[2,4,4,32,1152]{4,3,2,1,0:T(8,128)(2,1)}, bf16[2,4,4,32,1152]{4,3,2,1,0:T(8,128)(2,1)}, bf16[2,4,4,32,1152]{4,3,2,1,0:T(8,128)(2,1)}, bf16[2,4,4...) custom-call(bf16[144,256]{1,0:T(8,128)(2,1)} %refs_0_.1, ...), custom_call_target="tpu_custom_call" | custom-call | tf_op jit(solution)/shard_map/block/pallas_call | solution.py:671
  136.4 1.3 slice_bitcast_fusion
  137.7 1.4 fusion
  139.1 0.0 copy-start.1
  139.1 0.0 copy-start
  139.2 10.7 %widen.1 = (f32[1024,1152]{1,0:T(8,128)}, f32[1024,1152]{1,0:T(8,128)}, f32[1152,1024]{1,0:T(8,128)}, f32[1024,256]{1,0:T(8,128)}, f32[1024,128]{1,0:T(8,128)}, ...) custom-call(bf16[1024,1152]{1,0:T(8,128)(2,1)} %bitcast.13, bf16[1024,1152]{1,0:T(8,128)(2,1)} %bitcast.14, ...), custom_call_target="tpu_custom_call" | custom-call | tf_op jit(solution)/shard_map/widen/pallas_call | solution.py:693
  149.8 0.0 copy-done.1
  149.8 0.6 copy.29
  150.5 0.0 copy-done
  150.5 0.6 copy.30
  (2 shorter events, 0.0 us)
Async XLA Ops:
  139.1 10.7 %copy-start.1 = (bf16[144,256]{1,0:T(8,128)(2,1)S(1)}, bf16[144,256]{1,0:T(8,128)(2,1)}, u32[]{:S(2)}) copy-start(bf16[144,256]{1,0:T(8,128)(2,1)} %get-tuple-element.58) | copy-start | bytes 221188
  139.1 11.3 %copy-start = (bf16[144,256]{1,0:T(8,128)(2,1)S(1)}, bf16[144,256]{1,0:T(8,128)(2,1)}, u32[]{:S(2)}) copy-start(bf16[144,256]{1,0:T(8,128)(2,1)} %get-tuple-element.59) | copy-start | bytes 221188

commit v3 on v2

--- a/solution.py
+++ b/solution.py
@@ -1,3 +1,4 @@
+import math
 import functools
 import jax
 import jax.numpy as jnp
@@ -27,8 +28,8 @@
     lax.fori_loop(0, lead * per, add_step, 0)
 
 
-(T1P, T1M, I1P, I1M, M1P, M1M, T2P, T2M, I2P, I2M, M2P, M2M, Y, A2P, A2M, F2P, F2M, A1P, A1M, F1P, F1M) = range(21)
-KEYS = 21
+(T1P, T1M, I1P, I1M, M1P, M1M, T2P, T2M, I2P, I2M, M2P, M2M, Y, A2P, A2M, F2P, F2M, A1P, A1M, F1P, F1M, YA, YB, YC, YD) = range(25)
+KEYS = 25
 
 
 class Chunk:
@@ -51,6 +52,9 @@
         self.first = ((x, xp, xm), (z, zp, zm))
         self.second = ((z, zp, zm), (x, xp, xm))
         self.live = {}
+        R, C = src.shape[3:]
+        self.lo = (pl.ds(0, R // 2), pl.ds(0, C))
+        self.hi = (pl.ds(R // 2, R // 2), pl.ds(0, C))
 
     def go(self, h, name, src, dst, device):
         k = h * KEYS + name
@@ -94,28 +98,21 @@
             add_into(self.s1.at[h], (self.src.at[h, p], R.at[0], R.at[1]), self.step)
             p, plus, minus = self.second[h]
             k2, kp, km = lax.rem(p + 2, 4), lax.rem(p + 1, 4), lax.rem(p + 3, 4)
-            H, T, R = self.s1.at[h], self.t2.at[h], self.r2.at[h]
-            half = T.shape[1]
-            lo, hi = pl.ds(0, half), pl.ds(half, half)
-            self.go(h, T2P, H.at[k2, lo], T.at[0], plus)
-            self.go(h, T2M, H.at[k2, hi], T.at[1], minus)
-            self.go(h, I2P, H.at[kp, hi], R.at[0, hi], plus)
-            self.go(h, I2M, H.at[km, lo], R.at[1, lo], minus)
+            H, T, R, lo, hi = self.s1.at[h], self.t2.at[h], self.r2.at[h], self.lo, self.hi
+            self.go(h, T2P, H.at[(k2,) + lo], T.at[lo], plus)
+            self.go(h, T2M, H.at[(k2,) + hi], T.at[hi], minus)
+            self.go(h, I2P, H.at[(kp,) + hi], R.at[(0,) + hi], plus)
+            self.go(h, I2M, H.at[(km,) + lo], R.at[(1,) + lo], minus)
 
     def mid2(self):
         for h in range(2):
             p, plus, minus = self.second[h]
             kp, km = lax.rem(p + 1, 4), lax.rem(p + 3, 4)
-            H, T, R, M = self.s1.at[h], self.t2.at[h], self.r2.at[h], self.m2.at[h]
-            half = T.shape[1]
-            lo, hi = pl.ds(0, half), pl.ds(half, half)
-            step = min(self.step, half)
-            self.got(h, T2P)
-            add_into(M.at[pl.ds(0, 1)], (H.at[pl.ds(kp, 1), lo], T.at[pl.ds(0, 1)]), step)
-            self.go(h, M2P, M.at[0], R.at[0, lo], plus)
-            self.got(h, T2M)
-            add_into(M.at[pl.ds(1, 1)], (H.at[pl.ds(km, 1), hi], T.at[pl.ds(1, 1)]), step)
-            self.go(h, M2M, M.at[1], R.at[1, hi], minus)
+            R, own = self.r2.at[h], (pl.ds(h, 1),)
+            for name, arrived, k, part, slot, to in ((M2P, T2P, kp, self.lo, 0, plus), (M2M, T2M, km, self.hi, 1, minus)):
+                self.got(h, arrived)
+                add_into(self.m2.at[own + part], (self.s1.at[(h, pl.ds(k, 1)) + part], self.t2.at[own + part]), 16)
+                self.go(h, name, self.m2.at[(h,) + part], R.at[(slot,) + part], to)
 
     def fin2(self):
         for h in range(2):
@@ -140,12 +137,11 @@
             a = self.first[h][0]
             p, plus, minus = self.second[h]
             kp, km = lax.rem(p + 1, 4), lax.rem(p + 3, 4)
-            half = self.t2.shape[2]
             self.got(h, A2P)
-            blk = self.dst.at[h, a, km, pl.ds(0, half)]
+            blk = self.dst.at[(h, a, km) + self.lo]
             self.go(h, F2P, blk, blk, plus)
             self.got(h, A2M)
-            blk = self.dst.at[h, a, kp, pl.ds(half, half)]
+            blk = self.dst.at[(h, a, kp) + self.hi]
             self.go(h, F2M, blk, blk, minus)
 
     def ag1s(self):
@@ -177,6 +173,53 @@
         return [self.start1, self.mid1, self.fin1, self.mid2, self.fin2, self.finy, self.ag2, self.ag1s, self.ag1, self.end]
 
 
+class HalfChunk(Chunk):
+    def __init__(self, src, whole, *rest):
+        *_, where = rest
+        super().__init__(src, whole.at[where[0]], *rest)
+        R, C = src.shape[3:]
+        self.lo = (pl.ds(0, R), pl.ds(0, 640))
+        self.hi = (pl.ds(0, R), pl.ds(640, C - 640))
+
+    def fin2(self):
+        for h in range(2):
+            a = self.first[h][0]
+            p, plus, minus = self.second[h]
+            R = self.r2.at[h]
+            self.got(h, I2P, I2M, M2P, M2M)
+            add_into(self.dst.at[h, a, pl.ds(p, 1)], (self.s1.at[h, pl.ds(p, 1)], R.at[pl.ds(0, 1)], R.at[pl.ds(1, 1)]), self.step)
+            blk = self.dst.at[h, a, p]
+            self.go(h, A2P, blk, blk, plus)
+            self.go(h, A2M, blk, blk, minus)
+
+    def across(self, h, name, k):
+        blk = self.dst.at[h, k]
+        self.go(h, name, blk, blk, self.ynb)
+
+    def ag1s(self):
+        super().ag1s()
+        for h in range(2):
+            self.across(h, YA, self.first[h][0])
+
+    def ag1(self):
+        super().ag1()
+        for h in range(2):
+            p = self.first[h][0]
+            self.across(h, YB, lax.rem(p + 3, 4))
+            self.across(h, YC, lax.rem(p + 1, 4))
+
+    def last(self):
+        for h in range(2):
+            self.got(h, F1P, F1M)
+            self.across(h, YD, lax.rem(self.first[h][0] + 2, 4))
+
+    def end(self):
+        for h in range(2):
+            self.got(h, YA, YB, YC, YD)
+        for c in self.live.values():
+            c.wait_send()
+
+
 def coords():
     d = lax.axis_index("dp")
     return d // 16, (d // 4) % 4, d % 4
@@ -187,7 +230,7 @@
     bf = jnp.bfloat16
     return [
         pltpu.VMEM((2, 2, 2, R, C), bf), pltpu.VMEM((2, 2, 4, R, C), bf), pltpu.VMEM((2, 2, 2, R, C), bf), pltpu.VMEM((2, 4, R, C), bf),
-        pltpu.VMEM((2, 2, R // 2, C), bf), pltpu.VMEM((2, 2, R, C), bf), pltpu.VMEM((2, 2, R // 2, C), bf), pltpu.VMEM((2, R, C), bf), pltpu.VMEM((2, R, C), bf),
+        pltpu.VMEM((2, R, C), bf), pltpu.VMEM((2, 2, R, C), bf), pltpu.VMEM((2, R, C), bf), pltpu.VMEM((2, R, C), bf), pltpu.VMEM((2, R, C), bf),
         pltpu.SemaphoreType.DMA((2 * KEYS,)), pltpu.SemaphoreType.DMA((2 * KEYS,)),
     ]
 
@@ -336,24 +379,26 @@
     return jnp.concatenate([jnp.broadcast_to(c, (c.shape[0], 64)) for c in cols], axis=1)
 
 
-CHUNK_SHAPES = ((2, 4, 4, 32, 1152),) * 3 + ((2, 4, 4, 32, 768),)
+CHUNK_SHAPES = ((2, 4, 4, 16, 1152), (2, 4, 4, 32, 1152), (2, 4, 4, 32, 1152), (2, 4, 4, 32, 768))
+SUM_SHAPES = ((2,) + CHUNK_SHAPES[0],) + CHUNK_SHAPES[1:]
 
 
 def big_kernel(*refs):
     (
-        r_tokens, r_cotangent, r_lengths, r_frequency, r_attn_gain, r_mlp_gain, r_q_gain, r_k_gain,
+        r_tokens, r_cotangent, r_lengths, r_attn_gain, r_mlp_gain, r_q_gain, r_k_gain,
         r_w_query, r_w_key, r_w_value, r_w_output, h_gate, h_up, h_down,
-    ) = refs[:15]
-    h_sums, (r_vec_sum, r_block_out, r_input_grad) = refs[15:19], refs[19:22]
-    rest = refs[22:]
+    ) = refs[:14]
+    h_sums, (r_vec_sum, r_block_out, r_input_grad) = refs[14:18], refs[18:21]
+    rest = refs[21:]
     groups = [rest[NS * c:NS * c + NS] for c in range(4)]
     rest = rest[NS * 4:]
     small_refs, grads, sums, rest = rest[:4], rest[4:8], rest[8:12], rest[12:]
     (r_vec, r_d_two, r_own, r_d_one, r_gains, r_gains_sum, r_part, r_d_hidden, r_d_low, r_d_qkv) = rest[:10]
     (r_x, r_cot, r_normed_one, r_normed_two, r_attended, r_hidden, r_d_two_part, r_mlp_part) = rest[10:18]
     (r_q_low, r_k_low, r_v_low, r_q_plain, r_k_plain, r_q_inv, r_k_inv, r_cosine, r_sine, r_p, r_heads_out) = rest[18:29]
-    (r_act, r_d_gate, r_d_up, w_gate, w_up, w_down) = rest[29:35]
-    rest = rest[35:]
+    (r_acts, r_d_gate, r_d_up, w_gate, w_up, w_down, r_cots) = rest[29:36]
+    rest = rest[36:]
+    r_act = r_acts.at[pl.ds(0, 144)]
     ts, tb, tc, ta, td = rest[:4], rest[4:8], rest[8:12], rest[12:16], rest[16:19]
     sems, load_sem, store_sem = rest[19:21], rest[21], rest[22]
     where, place = coords(), tensor_place()
@@ -373,7 +418,8 @@
         pl.semaphore_signal(barrier, inc=1, device_id={"tensor": peer}, device_id_type=MESH)
     pl.semaphore_wait(barrier, len(peers) + 2)
 
-    c0, c1, c2, c3 = [Chunk(grads[c], sums[c], *groups[c], 16, where) for c in range(4)]
+    c0 = HalfChunk(grads[0], sums[0], *groups[0], 16, where)
+    c1, c2, c3 = [Chunk(grads[c], sums[c], *groups[c], 16, where) for c in range(1, 4)]
     r_attn = grads[3]
     small = SmallSum(where, r_vec, r_vec_sum, *small_refs)
     attended = sum_steps(r_part, r_attended, *ts, sems, 0, place, False)
@@ -433,8 +479,9 @@
         start = jnp.zeros(row.shape, jnp.int32)
         for end, length in zip(ends, one_length):
             start = start + jnp.where(row >= end, length, 0)
-        angles = (row - start).astype(f32) * r_frequency[...]
         lane = lax.broadcasted_iota(jnp.int32, (rows, 128), 1) % 64
+        power = (lane % 32).astype(f32) * (-2.0 / HEAD_SIZE)
+        angles = (row - start).astype(f32) * jnp.exp(power * math.log(THETA))
         cosine, sine = jnp.cos(angles), jnp.sin(angles)
         sine = jnp.where(lane < 32, -sine, sine)
         for k in (0, 128):
@@ -466,7 +513,7 @@
             plain = raw * inv
             inv_ref[...] = inv
             plain_ref[...] = plain
-            scaled = plain * gain[...]
+            scaled = plain * jnp.concatenate([gain[...]] * heads, axis=1)
             low[...] = (scaled * r_cosine[:, :width] + swap_halves(scaled) * r_sine[:, :width]).astype(bf)
         out = []
         for h in range(4):
@@ -519,7 +566,31 @@
 
         return lambda: lax.fori_loop(0, 4, tile, 0)
 
-    down_grad = weight_grad(r_cot, r_act, grads[0])
+    def swap_y(k, src, dst):
+        c = pltpu.make_async_remote_copy(
+            src_ref=src, dst_ref=dst, send_sem=sems[0].at[32 + k], recv_sem=sems[1].at[32 + k],
+            device_id={"dp": c0.ynb["dp"]}, device_id_type=MESH)
+        c.start()
+        moves[20 + k] = c
+
+    def swap_cot():
+        half = lambda v: pl.ds(pl.multiple_of(v * 512, 512), 512)
+        swap_y(0, r_cot.at[:, half(1 - y)], r_cots.at[pl.ds(144, 144)])
+        r_cots[0:144, :] = r_cot[:, half(y)]
+
+    def swap_act():
+        swap_y(1, r_act, r_acts.at[pl.ds(144, 144)])
+
+    def down_grad():
+        moves[20].wait()
+        moves[21].wait()
+
+        def tile(j, v):
+            grads[0][j] = dot_rows(r_cots[:, columns(j)], r_acts[...]).astype(bf).reshape(4, 4, 16, 1152)
+            return v
+
+        lax.fori_loop(0, 2, tile, 0)
+
     gate_grad = weight_grad(r_normed_two, r_d_gate, grads[1])
     up_grad = weight_grad(r_normed_two, r_d_up, grads[2])
 
@@ -602,7 +673,7 @@
             for h in range(1, heads):
                 total = total + sums[:, 64 * h:64 * h + 64]
             r_gains[0:1, place_at:place_at + 64] = total
-            u = turned * gain_ref[...]
+            u = turned * jnp.concatenate([gain_ref[...]] * heads, axis=1)
             inv = inv_ref[...]
             back = inv * (u - plain * spread(head_means(u * plain, heads), heads))
             r_d_qkv[:, put:put + width] = back.astype(jnp.bfloat16)
@@ -637,14 +708,14 @@
 
     for step in (
         gather_start, tables, lambda: gather_pass(0), lambda: gather_pass(1), lambda: gather_end(0),
-        attn_norm, attention, attended[0], lambda: gather_end(1), attended[1], attended[2], attended[3],
-        mlp_norm, mlp_units, down_grad, c0.start1, gate_grad, c1.start1, mlp_back, two[0], up_grad, two[1], c0.mid1, c2.start1,
-        mlp_out, two[2], own[0], two[3], own[1], own[2], c0.fin1, own[3], back_mlp_norm,
-        back_output, c1.mid1, back_scores, c0.mid2, back_head_norm, back_project,
-        one[0], gains[0], back_attn_weights, c3.start1, c0.fin2, one[1], gains[1], c1.fin1, c2.mid1, one[2], gains[2], c0.finy, one[3],
-        back_attn_norm, small.one, c1.mid2, c0.ag2, c2.fin1, c3.mid1, c1.fin2, small.two, c0.ag1s, c1.finy, c2.mid2, c3.fin1,
-        c1.ag2, c2.fin2, c3.mid2, small.three, c1.ag1s, c2.finy, c3.fin2, c0.ag1, c2.ag2, c3.finy, c2.ag1s, c3.ag2, small.four,
-        c3.ag1s, c1.ag1, leave(0, c0), c2.ag1, leave(1, c1), c3.ag1, leave(2, c2), leave(3, c3),
+        attn_norm, attention, attended[0], lambda: gather_end(1), attended[1], attended[2], swap_cot, attended[3],
+        mlp_norm, mlp_units, swap_act, gate_grad, c1.start1, mlp_back, two[0], up_grad, two[1], c2.start1, down_grad, c0.start1,
+        mlp_out, two[2], own[0], two[3], own[1], c1.mid1, own[2], c0.mid1, own[3], back_mlp_norm,
+        back_output, c2.mid1, c1.fin1, back_scores, c0.fin1, back_head_norm, back_project,
+        one[0], gains[0], back_attn_weights, c3.start1, c0.mid2, c1.mid2, one[1], gains[1], c0.fin2, c2.fin1, one[2], gains[2], c0.ag2, c1.fin2, one[3],
+        back_attn_norm, small.one, c0.ag1s, c3.mid1, c2.mid2, c1.finy, small.two, c0.ag1, c2.fin2, c3.fin1, c1.ag2, c0.last, c2.finy,
+        c3.mid2, small.three, c1.ag1s, c3.fin2, c2.ag2, c3.finy, c2.ag1s, c1.ag1, c3.ag2, small.four,
+        c3.ag1s, c2.ag1, leave(1, c1), c3.ag1, leave(0, c0), leave(2, c2), leave(3, c3),
     ):
         step()
     for out in stores:
@@ -655,27 +726,27 @@
     V, A = pl.BlockSpec(memory_space=pltpu.VMEM), pl.BlockSpec(memory_space=pl.ANY)
     f32, bf = jnp.float32, jnp.bfloat16
     S = jax.ShapeDtypeStruct
-    out_shape = [S(s, bf) for s in CHUNK_SHAPES] + [S((8, 1024), f32), S((144, 256), bf), S((144, 256), bf)]
+    out_shape = [S(s, bf) for s in SUM_SHAPES] + [S((8, 1024), f32), S((144, 256), bf), S((144, 256), bf)]
     B = lambda *shape: pltpu.VMEM(shape, bf)
     F = lambda *shape: pltpu.VMEM(shape, f32)
     D = lambda n: pltpu.SemaphoreType.DMA((n,))
     scratch = sum([scratch_for(s) for s in CHUNK_SHAPES], [])
     scratch += [F(3, 4, 8, 1024), F(3, 8, 1024), D(9), D(9)]
-    scratch += [B(*s) for s in CHUNK_SHAPES] * 2
+    scratch += [B(*s) for s in CHUNK_SHAPES] + [B(*s) for s in SUM_SHAPES]
     scratch += [F(8, 1024), B(144, 1024), F(144, 256), B(144, 1024), F(8, 128), F(8, 128), F(144, 1024), F(144, 1024), B(144, 1024), B(144, 512)]
     scratch += [B(144, 1024), B(144, 1024), B(144, 1024), B(144, 1024), B(144, 1024), F(144, 1024), F(144, 1024), F(144, 1024)]
     scratch += [B(144, 256), B(144, 128), B(144, 128), F(144, 256), F(144, 128), F(144, 256), F(144, 128), F(144, 256), F(144, 256), F(4, 144, 144), B(144, 256)]
-    scratch += [B(144, 1152), B(144, 1152), B(144, 1152), B(1024, 1152), B(1024, 1152), B(1152, 1024)]
+    scratch += [B(288, 1152), B(144, 1152), B(144, 1152), B(1024, 1152), B(1024, 1152), B(1152, 1024), B(288, 512)]
     scratch += ([B(144, 1024)] + [B(2, 144, 256)] * 3) * 4 + [F(8, 128)] * 3
-    scratch += [D(32), D(32), D(3), D(4)]
+    scratch += [D(34), D(34), D(3), D(4)]
     return pl.pallas_call(
-        big_kernel, out_shape=out_shape, in_specs=[V] * 12 + [A] * 3, out_specs=[A] * 4 + [V] * 3, scratch_shapes=scratch,
+        big_kernel, out_shape=out_shape, in_specs=[V] * 11 + [A] * 3, out_specs=[A] * 4 + [V] * 3, scratch_shapes=scratch,
         compiler_params=pltpu.CompilerParams(collective_id=0, has_side_effects=True, vmem_limit_bytes=61 * 1024 * 1024),
         name="block",
     )(*arrays)
 
 
-def widen_kernel(gate, up, down, attn, o_gate, o_up, o_down, o_q, o_k, o_v, o_out):
+def widen_kernel(gate, up, down, attn, vec, block, grad, o_gate, o_up, o_down, o_q, o_k, o_v, o_out, o_attn, o_mlp, o_qg, o_kg, o_block, o_grad):
     o_gate[...] = gate[...].astype(jnp.float32)
     o_up[...] = up[...].astype(jnp.float32)
     o_down[...] = down[...].astype(jnp.float32).T
@@ -685,19 +756,32 @@
     o_v[...] = wide[:, 384:512]
     o_out[...] = wide[:, 512:768].T
 
-
-def widen(gate, up, down, attn):
+    @pl.when(pl.program_id(0) == 0)
+    def _():
+        o_attn[...] = vec[0, :]
+        o_mlp[...] = vec[1, :]
+        o_qg[...] = vec[2, 0:64]
+        o_kg[...] = vec[2, 64:128]
+        o_block[...] = block[...]
+        o_grad[...] = grad[...]
+
+
+def widen(gate, up, down, attn, vec, block, grad):
     S = lambda *s: jax.ShapeDtypeStruct(s, jnp.float32)
     row = lambda w: pl.BlockSpec((128, w), lambda b: (b, 0))
     col = lambda h: pl.BlockSpec((h, 128), lambda b: (0, b))
+    all_of = lambda *s: pl.BlockSpec(s, lambda b: (0,) * len(s))
+    own = jax.ShapeDtypeStruct(block.shape, block.dtype)
     return pl.pallas_call(
         widen_kernel, grid=(8,),
-        in_specs=[row(1152), row(1152), row(1152), row(768)],
-        out_specs=[row(1152), row(1152), col(1152), row(256), row(128), row(128), col(256)],
-        out_shape=[S(1024, 1152), S(1024, 1152), S(1152, 1024), S(1024, 256), S(1024, 128), S(1024, 128), S(256, 1024)],
+        in_specs=[row(1152), row(1152), row(1152), row(768), all_of(8, 1024), all_of(144, 256), all_of(144, 256)],
+        out_specs=[row(1152), row(1152), col(1152), row(256), row(128), row(128), col(256),
+                   all_of(1024), all_of(1024), all_of(64), all_of(64), all_of(144, 256), all_of(144, 256)],
+        out_shape=[S(1024, 1152), S(1024, 1152), S(1152, 1024), S(1024, 256), S(1024, 128), S(1024, 128), S(256, 1024),
+                   S(1024), S(1024), S(64), S(64), own, own],
         compiler_params=pltpu.CompilerParams(vmem_limit_bytes=60 * 1024 * 1024),
         name="widen",
-    )(gate, up, down, attn)
+    )(gate, up, down, attn, vec, block, grad)
 
 
 EPS = 1e-05
@@ -732,17 +816,15 @@
     w_down,
     cotangent,
 ):
-    frequency = THETA ** (-jnp.arange(32, dtype=jnp.float32) * 2.0 / HEAD_SIZE)
     down, gate, up, attn, vec, block_out, input_grad = big(
         (
             tokens,
             cotangent,
             lengths,
-            jnp.tile(frequency[None], (1, 4)),
             attn_gain[None],
             mlp_gain[None],
-            jnp.tile(query_gain[None], (1, 4)),
-            jnp.tile(key_gain[None], (1, 2)),
+            query_gain[None],
+            key_gain[None],
             w_query,
             key_weight,
             value_weight,
@@ -752,24 +834,10 @@
             w_down,
         )
     )
-    gate, up, down, w_q, w_k, w_v, w_o = widen(
-        gate.reshape(1024, 1152), up.reshape(1024, 1152), down.reshape(1024, 1152), attn.reshape(1024, 768)
+    gate, up, down, w_q, w_k, w_v, w_o, attn_g, mlp_g, query_g, key_g, block_out, input_grad = widen(
+        gate.reshape(1024, 1152), up.reshape(1024, 1152), down.reshape(1024, 1152), attn.reshape(1024, 768), vec, block_out, input_grad
     )
-    return (
-        block_out,
-        input_grad,
-        vec[0],
-        w_q,
-        w_k,
-        w_v,
-        vec[2, :64],
-        vec[2, 64:128],
-        w_o,
-        vec[1],
-        gate,
-        up,
-        down,
-    )
+    return (block_out, input_grad, attn_g, w_q, w_k, w_v, query_g, key_g, w_o, mlp_g, gate, up, down)
 
 
 def solution(mesh):

time: 152 us -> 144 us (0.947)
  local copies, waits for them, and re-layouts: 7.2 us -> 0 us
    another operation x6 -> x0, local copies, waits for them, and re-layouts: 3.15 us -> none  [the longest x2 1.3 us: body(): jnp.tile(query_gain[None], (1, 4))]
where the time goes in v3:
time: 144 us; the launch traced here: 143 us
  Pallas kernels  143 us (99%)
    pallas_call x1, Pallas kernels, big(): pl.pallas_call(big_kernel, out_shape=out_shape, in_specs=[V] * 11 + [A] *...  132 us
    pallas_call x1, Pallas kernels, widen(): pl.pallas_call(widen_kernel, grid=(8,), in_specs=[row(1152), row(1152), r...  10.9 us

profile of v3, /device:TPU:0, one launch (start us, length us, event | category | flops | bytes accessed | tf_op | source)
XLA Modules:
  0.0 143.2 jit_solution(16427995464137933209)
XLA Ops:
  0.7 131.7 %block.1 = (bf16[2,2,4,4,16,1152]{5,4,3,2,1,0:T(8,128)(2,1)}, bf16[2,4,4,32,1152]{4,3,2,1,0:T(8,128)(2,1)}, bf16[2,4,4,32,1152]{4,3,2,1,0:T(8,128)(2,1)}, bf16[2...) custom-call(bf16[144,256]{1,0:T(8,128)(2,1)} %refs_0_.1, ...), custom_call_target="tpu_custom_call" | custom-call | tf_op jit(solution)/shard_map/block/pallas_call | solution.py:742
  132.3 10.9 %widen.1 = (f32[1024,1152]{1,0:T(8,128)}, f32[1024,1152]{1,0:T(8,128)}, f32[1152,1024]{1,0:T(8,128)}, f32[1024,256]{1,0:T(8,128)}, f32[1024,128]{1,0:T(8,128)}, ...) custom-call(bf16[1024,1152]{1,0:T(8,128)(2,1)} %bitcast.9, ...), custom_call_target="tpu_custom_call" | custom-call | tf_op jit(solution)/shard_map/widen/pallas_call | solution.py:775

commit v4 on v3

--- a/solution.py
+++ b/solution.py
@@ -196,13 +196,11 @@
         blk = self.dst.at[h, k]
         self.go(h, name, blk, blk, self.ynb)
 
-    def ag1s(self):
-        super().ag1s()
+    def ya(self):
         for h in range(2):
             self.across(h, YA, self.first[h][0])
 
-    def ag1(self):
-        super().ag1()
+    def ybc(self):
         for h in range(2):
             p = self.first[h][0]
             self.across(h, YB, lax.rem(p + 3, 4))
@@ -211,6 +209,9 @@
     def last(self):
         for h in range(2):
             self.got(h, F1P, F1M)
+
+    def yd(self):
+        for h in range(2):
             self.across(h, YD, lax.rem(self.first[h][0] + 2, 4))
 
     def end(self):
@@ -707,14 +708,13 @@
         r_input_grad[...] = r_d_hidden[:, mine].astype(jnp.bfloat16)
 
     for step in (
-        gather_start, tables, lambda: gather_pass(0), lambda: gather_pass(1), lambda: gather_end(0),
-        attn_norm, attention, attended[0], lambda: gather_end(1), attended[1], attended[2], swap_cot, attended[3],
-        mlp_norm, mlp_units, swap_act, gate_grad, c1.start1, mlp_back, two[0], up_grad, two[1], c2.start1, down_grad, c0.start1,
-        mlp_out, two[2], own[0], two[3], own[1], c1.mid1, own[2], c0.mid1, own[3], back_mlp_norm,
-        back_output, c2.mid1, c1.fin1, back_scores, c0.fin1, back_head_norm, back_project,
-        one[0], gains[0], back_attn_weights, c3.start1, c0.mid2, c1.mid2, one[1], gains[1], c0.fin2, c2.fin1, one[2], gains[2], c0.ag2, c1.fin2, one[3],
-        back_attn_norm, small.one, c0.ag1s, c3.mid1, c2.mid2, c1.finy, small.two, c0.ag1, c2.fin2, c3.fin1, c1.ag2, c0.last, c2.finy,
-        c3.mid2, small.three, c1.ag1s, c3.fin2, c2.ag2, c3.finy, c2.ag1s, c1.ag1, c3.ag2, small.four,
+        gather_start, tables, lambda: gather_pass(0), lambda: gather_pass(1), lambda: gather_end(0), attn_norm, attention, attended[0],
+        lambda: gather_end(1), attended[1], attended[2], swap_cot, attended[3], mlp_norm, mlp_units, swap_act, gate_grad, c1.start1,
+        mlp_back, two[0], up_grad, two[1], c2.start1, down_grad, c0.start1, mlp_out, two[2], own[0], two[3], own[1], c1.mid1, own[2],
+        c0.mid1, own[3], back_mlp_norm, back_output, c2.mid1, c1.fin1, back_scores, c0.fin1, back_head_norm, back_project, one[0],
+        gains[0], back_attn_weights, c3.start1, c0.mid2, c1.mid2, one[1], gains[1], c0.fin2, c2.fin1, one[2], gains[2], c0.ag2, c1.fin2,
+        one[3], back_attn_norm, small.one, c0.ag1s, c3.mid1, c2.mid2, c1.finy, small.two, c0.ag1, c2.fin2, c0.ya, c3.fin1, c1.ag2,
+        c2.finy, c3.mid2, small.three, c1.ag1s, c3.fin2, c0.ybc, c0.last, c0.yd, c2.ag2, c3.finy, c2.ag1s, c1.ag1, c3.ag2, small.four,
         c3.ag1s, c2.ag1, leave(1, c1), c3.ag1, leave(0, c0), leave(2, c2), leave(3, c3),
     ):
         step()

time: 144 us -> 132 us (0.917)
  Pallas kernels: 143 us -> 131 us
    pallas_call x1, Pallas kernels: 132 us -> 120 us  [big(): pl.pallas_call(big_kernel, out_shape=out_shape, in_specs=[V] * 11 + [A] *...]
where the time goes in v4:
time: 132 us; the launch traced here: 131 us
  Pallas kernels  131 us (99%)
    pallas_call x1, Pallas kernels, big(): pl.pallas_call(big_kernel, out_shape=out_shape, in_specs=[V] * 11 + [A] *...  120 us
    pallas_call x1, Pallas kernels, widen(): pl.pallas_call(widen_kernel, grid=(8,), in_specs=[row(1152), row(1152), r...  10.9 us

profile of v4, /device:TPU:0, one launch (start us, length us, event | category | flops | bytes accessed | tf_op | source)
XLA Modules:
  0.0 131.3 jit_solution(14257348144762470890)
XLA Ops:
  0.7 119.7 %block.1 = (bf16[2,2,4,4,16,1152]{5,4,3,2,1,0:T(8,128)(2,1)}, bf16[2,4,4,32,1152]{4,3,2,1,0:T(8,128)(2,1)}, bf16[2,4,4,32,1152]{4,3,2,1,0:T(8,128)(2,1)}, bf16[2...) custom-call(bf16[144,256]{1,0:T(8,128)(2,1)} %refs_0_.1, ...), custom_call_target="tpu_custom_call" | custom-call | tf_op jit(solution)/shard_map/block/pallas_call | solution.py:742
  120.4 10.9 %widen.1 = (f32[1024,1152]{1,0:T(8,128)}, f32[1024,1152]{1,0:T(8,128)}, f32[1152,1024]{1,0:T(8,128)}, f32[1024,256]{1,0:T(8,128)}, f32[1024,128]{1,0:T(8,128)}, ...) custom-call(bf16[1024,1152]{1,0:T(8,128)(2,1)} %bitcast.9, ...), custom_call_target="tpu_custom_call" | custom-call | tf_op jit(solution)/shard_map/widen/pallas_call | solution.py:775

commit v5 on v4

--- a/solution.py
+++ b/solution.py
@@ -70,13 +70,16 @@
 
     def start1(self):
         for h in range(2):
-            p, plus, minus = self.first[h]
-            k2, kp, km = lax.rem(p + 2, 4), lax.rem(p + 1, 4), lax.rem(p + 3, 4)
-            H, T, R = self.src.at[h], self.t1.at[h], self.r1.at[h]
-            self.go(h, T1P, H.at[k2, pl.ds(0, 2)], T.at[0], plus)
-            self.go(h, T1M, H.at[k2, pl.ds(2, 2)], T.at[1], minus)
-            self.go(h, I1P, H.at[kp, pl.ds(2, 2)], R.at[0, pl.ds(2, 2)], plus)
-            self.go(h, I1M, H.at[km, pl.ds(0, 2)], R.at[1, pl.ds(0, 2)], minus)
+            self.begin(h)
+
+    def begin(self, h):
+        p, plus, minus = self.first[h]
+        k2, kp, km = lax.rem(p + 2, 4), lax.rem(p + 1, 4), lax.rem(p + 3, 4)
+        H, T, R = self.src.at[h], self.t1.at[h], self.r1.at[h]
+        self.go(h, T1P, H.at[k2, pl.ds(0, 2)], T.at[0], plus)
+        self.go(h, T1M, H.at[k2, pl.ds(2, 2)], T.at[1], minus)
+        self.go(h, I1P, H.at[kp, pl.ds(2, 2)], R.at[0, pl.ds(2, 2)], plus)
+        self.go(h, I1M, H.at[km, pl.ds(0, 2)], R.at[1, pl.ds(0, 2)], minus)
 
     def mid1(self):
         for h in range(2):
@@ -271,26 +274,32 @@
         for s in range(2):
             live.append(send(low.at[:, columns(s * 2 + 1 - core)], near.at[s], sems, base + s, sib))
 
+    def fold(s):
+        mid[s] = (low[:, columns(s * 2 + core)].astype(jnp.float32) + near[s].astype(jnp.float32)).astype(jnp.bfloat16)
+
     def two():
-        order = (1 - side, side)
+        if scatter:
+            for s in range(2):
+                live[s].wait_recv()
+            fold(1 - side)
+            live.append(send(mid.at[1 - side], away.at[1 - side], sems, base + 2, far))
+            fold(side)
+            return
         for s in range(2):
             live[s].wait_recv()
-        for i, s in enumerate(order):
-            mid[s] = (low[:, columns(s * 2 + core)].astype(jnp.float32) + near[s].astype(jnp.float32)).astype(jnp.bfloat16)
-            if i == 0 or not scatter:
-                live.append(send(mid.at[s], away.at[s], sems, base + 2 + i, far))
+            fold(s)
+            live.append(send(mid.at[s], away.at[s], sems, base + 2 + s, far))
 
     def three():
         if scatter:
             live[2].wait_recv()
             out[...] = mid[side].astype(jnp.float32) + away[side].astype(jnp.float32)
             return
-        for i, s in enumerate((1 - side, side)):
-            live[2 + i].wait_recv()
-        for i, s in enumerate((1 - side, side)):
+        for s in range(2):
+            live[2 + s].wait_recv()
             there = out.at[:, columns(s * 2 + core)]
             out[:, columns(s * 2 + core)] = (mid[s].astype(jnp.float32) + away[s].astype(jnp.float32)).astype(jnp.bfloat16)
-            live.append(send(there, there, sems, base + 4 + i, sib))
+            live.append(send(there, there, sems, base + 4 + s, sib))
 
     def four():
         for c in live[4:]:
@@ -397,8 +406,8 @@
     (r_vec, r_d_two, r_own, r_d_one, r_gains, r_gains_sum, r_part, r_d_hidden, r_d_low, r_d_qkv) = rest[:10]
     (r_x, r_cot, r_normed_one, r_normed_two, r_attended, r_hidden, r_d_two_part, r_mlp_part) = rest[10:18]
     (r_q_low, r_k_low, r_v_low, r_q_plain, r_k_plain, r_q_inv, r_k_inv, r_cosine, r_sine, r_p, r_heads_out) = rest[18:29]
-    (r_acts, r_d_gate, r_d_up, w_gate, w_up, w_down, r_cots) = rest[29:36]
-    rest = rest[36:]
+    (r_acts, r_d_gate, r_d_up, w_gate, w_up, w_down, r_cots, r_d_act) = rest[29:37]
+    rest = rest[37:]
     r_act = r_acts.at[pl.ds(0, 144)]
     ts, tb, tc, ta, td = rest[:4], rest[4:8], rest[8:12], rest[12:16], rest[16:19]
     sems, load_sem, store_sem = rest[19:21], rest[21], rest[22]
@@ -541,8 +550,18 @@
 
         row_blocks(block, 0)
 
+    def back_down():
+        loads[2].wait()
+
+        def tile(j, v):
+            at = pl.ds(pl.multiple_of(j * 384, 128), 384)
+            r_d_act[:, at] = dot_last(r_cot[...], w_down[at, :])
+            return v
+
+        lax.fori_loop(0, 3, tile, 0)
+
     def mlp_units():
-        for load in loads:
+        for load in loads[:2]:
             load.wait()
 
         def tile(j, v):
@@ -552,20 +571,21 @@
             s = jax.nn.sigmoid(gate)
             silu = gate * s
             r_act[:, at] = (silu * up).astype(bf)
-            d_act = dot_last(r_cot[...], w_down[at, :])
+            d_act = r_d_act[:, at]
             r_d_gate[:, at] = (d_act * up * s * (1.0 + gate * (1.0 - s))).astype(bf)
             r_d_up[:, at] = (d_act * silu).astype(bf)
             return v
 
         lax.fori_loop(0, 3, tile, 0)
 
-    def weight_grad(left, right, out):
+    def weight_grad(left, right, out, h=None):
         def tile(j, v):
             part = dot_rows(left[:, columns(j)], right[...]).astype(bf)
             out[j // 2, pl.ds((j % 2) * 2, 2)] = part.reshape(2, 4, 32, right.shape[1])
             return v
 
-        return lambda: lax.fori_loop(0, 4, tile, 0)
+        first, last = (0, 4) if h is None else (2 * h, 2 * h + 2)
+        return lambda: lax.fori_loop(first, last, tile, 0)
 
     def swap_y(k, src, dst):
         c = pltpu.make_async_remote_copy(
@@ -592,7 +612,7 @@
 
         lax.fori_loop(0, 2, tile, 0)
 
-    gate_grad = weight_grad(r_normed_two, r_d_gate, grads[1])
+    gate_low, gate_high = [weight_grad(r_normed_two, r_d_gate, grads[1], h) for h in range(2)]
     up_grad = weight_grad(r_normed_two, r_d_up, grads[2])
 
     def mlp_back():
@@ -709,13 +729,14 @@
 
     for step in (
         gather_start, tables, lambda: gather_pass(0), lambda: gather_pass(1), lambda: gather_end(0), attn_norm, attention, attended[0],
-        lambda: gather_end(1), attended[1], attended[2], swap_cot, attended[3], mlp_norm, mlp_units, swap_act, gate_grad, c1.start1,
-        mlp_back, two[0], up_grad, two[1], c2.start1, down_grad, c0.start1, mlp_out, two[2], own[0], two[3], own[1], c1.mid1, own[2],
-        c0.mid1, own[3], back_mlp_norm, back_output, c2.mid1, c1.fin1, back_scores, c0.fin1, back_head_norm, back_project, one[0],
-        gains[0], back_attn_weights, c3.start1, c0.mid2, c1.mid2, one[1], gains[1], c0.fin2, c2.fin1, one[2], gains[2], c0.ag2, c1.fin2,
-        one[3], back_attn_norm, small.one, c0.ag1s, c3.mid1, c2.mid2, c1.finy, small.two, c0.ag1, c2.fin2, c0.ya, c3.fin1, c1.ag2,
-        c2.finy, c3.mid2, small.three, c1.ag1s, c3.fin2, c0.ybc, c0.last, c0.yd, c2.ag2, c3.finy, c2.ag1s, c1.ag1, c3.ag2, small.four,
-        c3.ag1s, c2.ag1, leave(1, c1), c3.ag1, leave(0, c0), leave(2, c2), leave(3, c3),
+        lambda: gather_end(1), attended[1], back_down, attended[2], swap_cot, attended[3], mlp_norm, mlp_units, swap_act, gate_low,
+        lambda: c1.begin(0), gate_high, lambda: c1.begin(1), mlp_back, two[0], up_grad, two[1], c2.start1, down_grad, c0.start1, mlp_out,
+        two[2], own[0], two[3], own[1], c1.mid1, own[2], c0.mid1, own[3], back_mlp_norm, back_output, c2.mid1, c1.fin1, back_scores,
+        c0.fin1, back_head_norm, back_project, one[0], gains[0], back_attn_weights, c3.start1, c0.mid2, c1.mid2, one[1], gains[1],
+        c0.fin2, c2.fin1, one[2], gains[2], c0.ag2, c1.fin2, one[3], back_attn_norm, small.one, c0.ag1s, c3.mid1, c2.mid2, c1.finy,
+        small.two, c0.ag1, c2.fin2, c0.ya, c3.fin1, c1.ag2, c2.finy, c3.mid2, small.three, c1.ag1s, c3.fin2, c0.ybc, c0.last, c0.yd,
+        c2.ag2, c3.finy, c2.ag1s, c1.ag1, c3.ag2, small.four, c3.ag1s, c2.ag1, leave(1, c1), c3.ag1, leave(0, c0), leave(2, c2), leave(3,
+        c3),
     ):
         step()
     for out in stores:
@@ -736,7 +757,7 @@
     scratch += [F(8, 1024), B(144, 1024), F(144, 256), B(144, 1024), F(8, 128), F(8, 128), F(144, 1024), F(144, 1024), B(144, 1024), B(144, 512)]
     scratch += [B(144, 1024), B(144, 1024), B(144, 1024), B(144, 1024), B(144, 1024), F(144, 1024), F(144, 1024), F(144, 1024)]
     scratch += [B(144, 256), B(144, 128), B(144, 128), F(144, 256), F(144, 128), F(144, 256), F(144, 128), F(144, 256), F(144, 256), F(4, 144, 144), B(144, 256)]
-    scratch += [B(288, 1152), B(144, 1152), B(144, 1152), B(1024, 1152), B(1024, 1152), B(1152, 1024), B(288, 512)]
+    scratch += [B(288, 1152), B(144, 1152), B(144, 1152), B(1024, 1152), B(1024, 1152), B(1152, 1024), B(288, 512), F(144, 1152)]
     scratch += ([B(144, 1024)] + [B(2, 144, 256)] * 3) * 4 + [F(8, 128)] * 3
     scratch += [D(34), D(34), D(3), D(4)]
     return pl.pallas_call(
@@ -768,12 +789,12 @@
 
 def widen(gate, up, down, attn, vec, block, grad):
     S = lambda *s: jax.ShapeDtypeStruct(s, jnp.float32)
-    row = lambda w: pl.BlockSpec((128, w), lambda b: (b, 0))
-    col = lambda h: pl.BlockSpec((h, 128), lambda b: (0, b))
+    row = lambda w: pl.BlockSpec((256, w), lambda b: (b, 0))
+    col = lambda h: pl.BlockSpec((h, 256), lambda b: (0, b))
     all_of = lambda *s: pl.BlockSpec(s, lambda b: (0,) * len(s))
     own = jax.ShapeDtypeStruct(block.shape, block.dtype)
     return pl.pallas_call(
-        widen_kernel, grid=(8,),
+        widen_kernel, grid=(4,),
         in_specs=[row(1152), row(1152), row(1152), row(768), all_of(8, 1024), all_of(144, 256), all_of(144, 256)],
         out_specs=[row(1152), row(1152), col(1152), row(256), row(128), row(128), col(256),
                    all_of(1024), all_of(1024), all_of(64), all_of(64), all_of(144, 256), all_of(144, 256)],

time: 132 us -> 130 us (0.985)
  Pallas kernels: 131 us -> 129 us
where the time goes in v5:
time: 130 us
  Pallas kernels  129 us (99%)
    pallas_call x1, Pallas kernels, big(): pl.pallas_call(big_kernel, out_shape=out_shape, in_specs=[V] * 11 + [A] *...  119 us
    pallas_call x1, Pallas kernels, widen(): pl.pallas_call(widen_kernel, grid=(4,), in_specs=[row(1152), row(1152), r...  10.1 us

profile of v5, /device:TPU:0, one launch (start us, length us, event | category | flops | bytes accessed | tf_op | source)
XLA Modules:
  0.0 129.6 jit_solution(14977219913313647179)
XLA Ops:
  0.7 118.8 %block.1 = (bf16[2,2,4,4,16,1152]{5,4,3,2,1,0:T(8,128)(2,1)}, bf16[2,4,4,32,1152]{4,3,2,1,0:T(8,128)(2,1)}, bf16[2,4,4,32,1152]{4,3,2,1,0:T(8,128)(2,1)}, bf16[2...) custom-call(bf16[144,256]{1,0:T(8,128)(2,1)} %refs_0_.1, ...), custom_call_target="tpu_custom_call" | custom-call | tf_op jit(solution)/shard_map/block/pallas_call | solution.py:763
  119.5 10.1 %widen.1 = (f32[1024,1152]{1,0:T(8,128)}, f32[1024,1152]{1,0:T(8,128)}, f32[1152,1024]{1,0:T(8,128)}, f32[1024,256]{1,0:T(8,128)}, f32[1024,128]{1,0:T(8,128)}, ...) custom-call(bf16[1024,1152]{1,0:T(8,128)(2,1)} %bitcast.9, ...), custom_call_target="tpu_custom_call" | custom-call | tf_op jit(solution)/shard_map/widen/pallas_call | solution.py:796

commit v6 on v5

--- a/solution.py
+++ b/solution.py
@@ -789,12 +789,12 @@
 
 def widen(gate, up, down, attn, vec, block, grad):
     S = lambda *s: jax.ShapeDtypeStruct(s, jnp.float32)
-    row = lambda w: pl.BlockSpec((256, w), lambda b: (b, 0))
-    col = lambda h: pl.BlockSpec((h, 256), lambda b: (0, b))
+    row = lambda w: pl.BlockSpec((512, w), lambda b: (b, 0))
+    col = lambda h: pl.BlockSpec((h, 512), lambda b: (0, b))
     all_of = lambda *s: pl.BlockSpec(s, lambda b: (0,) * len(s))
     own = jax.ShapeDtypeStruct(block.shape, block.dtype)
     return pl.pallas_call(
-        widen_kernel, grid=(4,),
+        widen_kernel, grid=(2,),
         in_specs=[row(1152), row(1152), row(1152), row(768), all_of(8, 1024), all_of(144, 256), all_of(144, 256)],
         out_specs=[row(1152), row(1152), col(1152), row(256), row(128), row(128), col(256),
                    all_of(1024), all_of(1024), all_of(64), all_of(64), all_of(144, 256), all_of(144, 256)],

time: 130 us -> 129 us (level)
  no operation moved by 1% of the time
where the time goes in v6:
time: 129 us
  Pallas kernels  128 us (99%)
    pallas_call x1, Pallas kernels, big(): pl.pallas_call(big_kernel, out_shape=out_shape, in_specs=[V] * 11 + [A] *...  119 us
    pallas_call x1, Pallas kernels, widen(): pl.pallas_call(widen_kernel, grid=(2,), in_specs=[row(1152), row(1152), r...  9.51 us

profile of v6, /device:TPU:0, one launch (start us, length us, event | category | flops | bytes accessed | tf_op | source)
XLA Modules:
  0.0 129.0 jit_solution(3672307224144571979)
XLA Ops:
  0.7 118.8 %block.1 = (bf16[2,2,4,4,16,1152]{5,4,3,2,1,0:T(8,128)(2,1)}, bf16[2,4,4,32,1152]{4,3,2,1,0:T(8,128)(2,1)}, bf16[2,4,4,32,1152]{4,3,2,1,0:T(8,128)(2,1)}, bf16[2...) custom-call(bf16[144,256]{1,0:T(8,128)(2,1)} %refs_0_.1, ...), custom_call_target="tpu_custom_call" | custom-call | tf_op jit(solution)/shard_map/block/pallas_call | solution.py:763
  119.5 9.5 %widen.1 = (f32[1024,1152]{1,0:T(8,128)}, f32[1024,1152]{1,0:T(8,128)}, f32[1152,1024]{1,0:T(8,128)}, f32[1024,256]{1,0:T(8,128)}, f32[1024,128]{1,0:T(8,128)}, ...) custom-call(bf16[1024,1152]{1,0:T(8,128)(2,1)} %bitcast.9, ...), custom_call_target="tpu_custom_call" | custom-call | tf_op jit(solution)/shard_map/widen/pallas_call | solution.py:796
